TPU v7x, 32 devices: a whole 2x2x4 slice. The times are simulated.
32 devices in a mesh: gx: 8 (over y, x, core), gy: 4 (over z).
Axes of the slice: x: 2, y: 2, z: 4, core: 2. Of those that a mesh axis runs over, the one named last changes fastest.
Arguments:
- right_side: bfloat16 [8, 4, 896, 128], P('gx', 'gy')
- schur_offdiag: bfloat16 [8, 4, 896, 896], P('gx', 'gy'), may hold values from -0.125 to 0.125
- schur_diag: float32 [8, 4, 896], P('gx', 'gy'), may hold values from 1.5 to 3
- trace_offdiag: bfloat16 [8, 4, 896, 896], P('gx', 'gy'), may hold values from -0.0390625 to 0.0390625
- trace_diag: float32 [8, 4, 896], P('gx', 'gy'), may hold values from 0.3 to 0.7
- couplings: bfloat16 [8, 4, 4, 128, 128], P('gx', 'gy'), may hold values from -0.375 to 0.375
- margin_rows: int32 [8, 4, 4, 128], P('gx', 'gy'), may hold values from 0 to 895, as said below
- deflation: bfloat16 [8, 4, 8, 896], P('gx', 'gy'), may hold values from -0.59765625 to 0.59765625
- coarse_inverse: float32 [256, 256], P(('gx', 'gy'))
- coarse_map: int32 [256], replicated, may hold values from 0 to 255, each once
Outputs:
- solution: float32 [8, 4, 896, 128], P('gx', 'gy')
- residual: float32 [8, 4, 896, 128], P('gx', 'gy')
Inputs may be any that keep to these rules, and one draw needn't show every extreme that they name: `margin_rows`: the 512 rows of one subdomain's four lists are all distinct. `coarse_map`: every coarse number appears once.
All inputs are finite; a program needn't handle non-finite values.
Results may differ from a plain program's by a relative error of at most 0.022.
Values may be sent and summed in bfloat16 or wider, within the bound.
A program may use at most 64 MiB of HBM per device.

v0:
```python
import jax
import jax.numpy as jnp
from jax import lax
from jax.sharding import PartitionSpec as P

ITERS = 3


def from_behind(value, axis, steps):
    count = lax.axis_size(axis)
    leading, last = (max(0, -steps), min(count, count - steps))
    return lax.ppermute(value, axis, [(source, source + steps) for source in range(leading, last)])


def pass_columns(rows, offset):
    return from_behind(rows, "gx", offset)


def pass_lines(rows, offset):
    return from_behind(rows, "gy", offset)


def shards(
    right_side,
    schur_offdiag,
    schur_diag,
    trace_offdiag,
    trace_diag,
    couplings,
    margin_rows,
    deflation,
    coarse_inverse,
    coarse_map,
):
    rhs_wide = right_side[0, 0].astype(jnp.float32)
    schur_mat = schur_offdiag[0, 0]
    schur_scale = schur_diag[0, 0][:, None]
    trace_mat = trace_offdiag[0, 0]
    trace_scale = trace_diag[0, 0][:, None]
    coupling_blocks = couplings[0, 0]
    rows_lists = margin_rows[0, 0]
    flat_rows = rows_lists.reshape(-1)
    vectors = deflation[0, 0]
    vectors_wide = vectors.astype(jnp.float32).T
    coarse_cols = jnp.take(coarse_inverse, coarse_map, axis=1)

    def apply_schur(field):
        rounded = lax.optimization_barrier(field.astype(jnp.bfloat16))
        result = schur_scale * rounded.astype(jnp.float32) + jnp.dot(
            schur_mat, rounded, preferred_element_type=jnp.float32
        )
        sent_rows = rounded[rows_lists]
        received = jnp.stack(
            [
                pass_columns(sent_rows[1], 1),
                pass_columns(sent_rows[0], -1),
                pass_lines(sent_rows[3], 1),
                pass_lines(sent_rows[2], -1),
            ]
        )
        coupled = jnp.einsum(
            "dab,dbs->das", coupling_blocks, received, preferred_element_type=jnp.float32
        )
        return result.at[flat_rows].add(-coupled.reshape(-1, coupled.shape[-1]))

    def apply_prec(field):
        rounded = lax.optimization_barrier(field.astype(jnp.bfloat16))
        result = trace_scale * rounded.astype(jnp.float32) + jnp.dot(
            trace_mat, rounded, preferred_element_type=jnp.float32
        )
        coarse = jnp.dot(vectors, rounded, preferred_element_type=jnp.float32)
        stacked = lax.all_gather(coarse, ("gx", "gy"), axis=0, tiled=True)
        solved = jnp.dot(coarse_cols, stacked, precision=lax.Precision.HIGHEST)
        return result + jnp.dot(vectors_wide, solved, precision=lax.Precision.HIGHEST)

    solution = jnp.zeros(rhs_wide.shape, jnp.float32)
    direction = apply_prec(rhs_wide)
    for iteration in range(ITERS):
        image = apply_schur(direction)
        mapped = apply_prec(image)
        numer, denom = lax.psum(
            (jnp.sum(mapped * direction, axis=0), jnp.sum(mapped * mapped, axis=0)), ("gx", "gy")
        )
        alpha = numer / denom
        solution = solution + alpha * direction
        direction = direction - alpha * mapped
    residual = rhs_wide - apply_schur(solution)
    return (solution[None, None], residual[None, None])


def solution(mesh):
    return jax.shard_map(
        shards,
        mesh=mesh,
        in_specs=(
            P("gx", "gy", None, None),
            P("gx", "gy", None, None),
            P("gx", "gy", None),
            P("gx", "gy", None, None),
            P("gx", "gy", None),
            P("gx", "gy", None, None, None),
            P("gx", "gy", None, None),
            P("gx", "gy", None, None),
            P(("gx", "gy"), None),
            P(),
        ),
        out_specs=(P("gx", "gy", None, None), P("gx", "gy", None, None)),
        check_vma=False,
    )
```

profile of v0, /device:TPU:0, one launch (start us, length us, event | category | flops | bytes accessed | tf_op | source)
XLA Modules:
  0.0 498.5 jit_solution(13269913649326509001)
XLA Ops:
  3.9 70.7 %all_gather.12 = f32[256,128]{1,0:T(8,128)S(1)} all-gather(f32[8,128]{1,0:T(8,128)S(1)} %fusion.129), channel_id=1, replica_groups=mesh['gx'=8,'gy'=4] {'gx','gy'}, dimensions={0}, use_global_device_ids=true | all-gather | bytes 135168 | tf_op jit(solution)/shard_map/all_gather | solution.py:72
  76.6 1.9 convolution_bitcast_fusion.3
  79.3 2.7 fusion.146
  81.9 1.9 gather_fusion.1
  83.8 1.4 fusion.145
  85.3 1.9 collective-permute-start
  87.2 1.9 collective-permute-start.2
  93.1 3.4 collective-permute-done.3
  96.4 1.7 convolution_negate_fusion.3
  98.1 5.2 %scatter_fusion = f32[896,128]{1,0:T(8,128)} fusion(f32[896,128]{1,0:T(8,128)} %fusion.37, s32[512]{0:T(512)S(1)} %bitcast.204, f32[512,128]{1,0:T(8,128)} %bitcast.201), kind=kCustom, calls=%fused_computation.5 | custom fusion | flops 65536 | bytes 788480 | tf_op jit(solution)/shard_map/scatter-add | solution.py:64
  104.6 65.2 %all_gather.13 = f32[256,128]{1,0:T(8,128)S(1)} all-gather(f32[8,128]{1,0:T(8,128)S(1)} %convolution_bitcast_fusion.6), channel_id=1, replica_groups=mesh['gx'=8,'gy'=4] {'gx','gy'}, dimensions={0}, use_global_device_ids=true | all-gather | bytes 135168 | tf_op jit(solution)/shard_map/all_gather | solution.py:72
  170.6 1.4 multiply_reduce_fusion.4
  172.0 40.8 %all-reduce.2 = (f32[128]{0:T(128)S(1)}, f32[128]{0:T(128)S(1)}) all-reduce(f32[128]{0:T(128)S(1)} %get-tuple-element.7, f32[128]{0:T(128)S(1)} %get-tuple-element.6), channel_id=1, replica_groups=mesh['gx'=8,'gy'=4] {'gx','gy'}, use_global_device_ids=true, to_apply=%region_2.3 | all-reduce | flops 256 | bytes 2048 | tf_op jit(solution)/shard_map/psum | solution.py:81
  212.8 2.0 fusion.141
  214.8 1.9 gather_fusion.2
  218.8 1.8 collective-permute-start.6
  226.0 1.8 collective-permute-done.7
  228.6 5.2 %scatter_fusion.1 = f32[896,128]{1,0:T(8,128)} fusion(f32[896,128]{1,0:T(8,128)} %fusion.40, s32[512]{0:T(512)S(1)} %bitcast.205, f32[512,128]{1,0:T(8,128)} %bitcast.202), kind=kCustom, calls=%fused_computation.6 | custom fusion | flops 65536 | bytes 788480 | tf_op jit(solution)/shard_map/scatter-add | solution.py:64
  235.1 69.6 %all_gather.14 = f32[256,128]{1,0:T(8,128)S(1)} all-gather(f32[8,128]{1,0:T(8,128)S(1)} %convolution_bitcast_fusion.5), channel_id=1, replica_groups=mesh['gx'=8,'gy'=4] {'gx','gy'}, dimensions={0}, use_global_device_ids=true | all-gather | bytes 135168 | tf_op jit(solution)/shard_map/all_gather | solution.py:72
  305.6 1.4 multiply_reduce_fusion.2
  307.0 38.7 %all-reduce.1 = (f32[128]{0:T(128)S(1)}, f32[128]{0:T(128)S(1)}) all-reduce(f32[128]{0:T(128)S(1)} %get-tuple-element.5, f32[128]{0:T(128)S(1)} %get-tuple-element.4), channel_id=1, replica_groups=mesh['gx'=8,'gy'=4] {'gx','gy'}, use_global_device_ids=true, to_apply=%region_7.8 | all-reduce | flops 256 | bytes 2048 | tf_op jit(solution)/shard_map/psum | solution.py:81
  346.9 1.9 gather_fusion.3
  351.0 3.1 collective-permute-start.10
  359.4 1.8 collective-permute-done.11
  362.1 5.2 %scatter_fusion.2 = f32[896,128]{1,0:T(8,128)} fusion(f32[896,128]{1,0:T(8,128)} %fusion.43, s32[512]{0:T(512)S(1)} %bitcast.206, f32[512,128]{1,0:T(8,128)} %bitcast.203), kind=kCustom, calls=%fused_computation.7 | custom fusion | flops 65536 | bytes 788480 | tf_op jit(solution)/shard_map/scatter-add | solution.py:64
  368.5 68.4 %all_gather.15 = f32[256,128]{1,0:T(8,128)S(1)} all-gather(f32[8,128]{1,0:T(8,128)S(1)} %convolution_bitcast_fusion.4), channel_id=1, replica_groups=mesh['gx'=8,'gy'=4] {'gx','gy'}, dimensions={0}, use_global_device_ids=true | all-gather | bytes 135168 | tf_op jit(solution)/shard_map/all_gather | solution.py:72
  438.5 39.8 %all-reduce = (f32[128]{0:T(128)S(1)}, f32[128]{0:T(128)S(1)}) all-reduce(f32[128]{0:T(128)S(1)} %get-tuple-element.3, f32[128]{0:T(128)S(1)} %get-tuple-element.2), channel_id=1, replica_groups=mesh['gx'=8,'gy'=4] {'gx','gy'}, use_global_device_ids=true, to_apply=%region_12.13 | all-reduce | flops 256 | bytes 2048 | tf_op jit(solution)/shard_map/psum | solution.py:81
  478.3 2.2 fusion.140
  480.5 1.9 gather_fusion.4
  484.6 2.3 collective-permute-start.14
  492.2 1.8 collective-permute-done.15
  494.2 3.5 scatter_fusion.3
  (101 shorter events, 43.4 us)
Async XLA Ops:
  0.6 78.6 %copy-start = (bf16[1,1,896,896]{3,2,1,0:T(8,128)(2,1)S(1)}, bf16[1,1,896,896]{3,2,1,0:T(8,128)(2,1)}, u32[]{:S(2)}) copy-start(bf16[1,1,896,896]{3,2,1,0:T(8,128)(2,1)} %param.13) | copy-start | bytes 4816900
  79.2 12.4 %copy-start.14 = (f32[1,1,896]{2,1,0:T(1,128)S(1)}, f32[1,1,896]{2,1,0:T(1,128)}, u32[]{:S(2)}) copy-start(f32[1,1,896]{2,1,0:T(1,128)} %param.12) | copy-start | bytes 10756
  79.3 12.4 %copy-start.1 = (bf16[1,1,896,896]{3,2,1,0:T(8,128)(2,1)S(1)}, bf16[1,1,896,896]{3,2,1,0:T(8,128)(2,1)}, u32[]{:S(2)}) copy-start(bf16[1,1,896,896]{3,2,1,0:T(8,128)(2,1)} %param.11) | copy-start | bytes 4816900
  81.9 11.1 %copy-start.13 = (s32[1,1,4,128]{3,2,1,0:T(4,128)S(1)}, s32[1,1,4,128]{3,2,1,0:T(4,128)}, u32[]{:S(2)}) copy-start(s32[1,1,4,128]{3,2,1,0:T(4,128)} %param.16) | copy-start | bytes 6148
  85.3 7.8 %collective-permute-start = (bf16[128,128]{1,0:T(8,128)(2,1)}, bf16[128,128]{1,0:T(8,128)(2,1)}, u32[]{:S(2)}, u32[]{:S(2)}) collective-permute-start(bf16[128,128]{1,0:T(8,128)(2,1)} %get-tuple-element.30), channel_id=1, source_target_pairs={{0,4},{4,8},{8,12},{12,16},{16,20},{20,24},{24,28},{1,5},{5,9},{9,... | collective-permute-start | bytes 98312 | tf_op jit(solution)/shard_map/ppermute | solution.py:12
  87.2 5.9 %collective-permute-start.2 = (bf16[128,128]{1,0:T(8,128)(2,1)}, bf16[128,128]{1,0:T(8,128)(2,1)}, u32[]{:S(2)}, u32[]{:S(2)}) collective-permute-start(bf16[128,128]{1,0:T(8,128)(2,1)} %get-tuple-element.31), channel_id=1, source_target_pairs={{0,1},{1,2},{2,3},{4,5},{5,6},{6,7},{8,9},{9,10},{10,11},{12,13},{... | collective-permute-start | bytes 98312 | tf_op jit(solution)/shard_map/ppermute | solution.py:12
  89.0 4.0 collective-permute-start.1
  90.3 6.1 %collective-permute-start.3 = (bf16[128,128]{1,0:T(8,128)(2,1)S(1)}, bf16[128,128]{1,0:T(8,128)(2,1)}, u32[]{:S(2)}, u32[]{:S(2)}) collective-permute-start(bf16[128,128]{1,0:T(8,128)(2,1)S(1)} %get-tuple-element.33), channel_id=1, source_target_pairs={{1,0},{2,1},{3,2},{5,4},{6,5},{7,6},{9,8},{10,9},{11,10},{13,12},{... | collective-permute-start | bytes 98312 | tf_op jit(solution)/shard_map/ppermute | solution.py:12
  91.7 4.8 copy-start.15
  98.1 6.3 %copy-start.12 = (bf16[1,1,8,896]{3,2,1,0:T(8,128)(2,1)S(1)}, bf16[1,1,8,896]{3,2,1,0:T(8,128)(2,1)}, u32[]{:S(2)}) copy-start(bf16[1,1,8,896]{3,2,1,0:T(8,128)(2,1)} %param.17) | copy-start | bytes 43012
  98.1 71.6 %copy-start.8 = (f32[256,8]{1,0:T(8,128)S(1)}, f32[256,8]{1,0:T(8,128)}, u32[]{:S(2)}) copy-start(f32[256,8]{1,0:T(8,128)} %copy-done.7) | copy-start | bytes 24580
  103.3 67.3 %copy-start.6 = (f32[896,128]{1,0:T(8,128)S(1)}, f32[896,128]{1,0:T(8,128)}, u32[]{:S(2)}) copy-start(f32[896,128]{1,0:T(8,128)} %get-tuple-element.35) | copy-start | bytes 1376260
  216.7 11.1 %copy-start.16 = (bf16[1,1,4,128,128]{4,3,2,1,0:T(8,128)(2,1)S(1)}, bf16[1,1,4,128,128]{4,3,2,1,0:T(8,128)(2,1)}, u32[]{:S(2)}) copy-start(bf16[1,1,4,128,128]{4,3,2,1,0:T(8,128)(2,1)} %param.15) | copy-start | bytes 393220
  217.5 7.1 %collective-permute-start.4 = (bf16[128,128]{1,0:T(8,128)(2,1)S(1)}, bf16[128,128]{1,0:T(8,128)(2,1)S(1)}, u32[]{:S(2)}, u32[]{:S(2)}) collective-permute-start(bf16[128,128]{1,0:T(8,128)(2,1)S(1)} %get-tuple-element.26), channel_id=1, source_target_pairs={{0,4},{4,8},{8,12},{12,16},{16,20},{20,24},{24,28},{1,5},{5,9},{9,... | collective-permute-start | bytes 98312 | tf_op jit(solution)/shard_map/ppermute | solution.py:12
  218.8 5.8 %collective-permute-start.6 = (bf16[128,128]{1,0:T(8,128)(2,1)S(1)}, bf16[128,128]{1,0:T(8,128)(2,1)S(1)}, u32[]{:S(2)}, u32[]{:S(2)}) collective-permute-start(bf16[128,128]{1,0:T(8,128)(2,1)S(1)} %get-tuple-element.27), channel_id=1, source_target_pairs={{0,1},{1,2},{2,3},{4,5},{5,6},{6,7},{8,9},{9,10},{10,11},{12,13},{... | collective-permute-start | bytes 98312 | tf_op jit(solution)/shard_map/ppermute | solution.py:12
  220.6 5.3 %collective-permute-start.5 = (bf16[128,128]{1,0:T(8,128)(2,1)S(1)}, bf16[128,128]{1,0:T(8,128)(2,1)S(1)}, u32[]{:S(2)}, u32[]{:S(2)}) collective-permute-start(bf16[128,128]{1,0:T(8,128)(2,1)S(1)} %get-tuple-element.28), channel_id=1, source_target_pairs={{4,0},{8,4},{12,8},{16,12},{20,16},{24,20},{28,24},{5,1},{9,5},{13... | collective-permute-start | bytes 98312 | tf_op jit(solution)/shard_map/ppermute | solution.py:12
  221.9 5.8 %collective-permute-start.7 = (bf16[128,128]{1,0:T(8,128)(2,1)S(1)}, bf16[128,128]{1,0:T(8,128)(2,1)S(1)}, u32[]{:S(2)}, u32[]{:S(2)}) collective-permute-start(bf16[128,128]{1,0:T(8,128)(2,1)S(1)} %get-tuple-element.29), channel_id=1, source_target_pairs={{1,0},{2,1},{3,2},{5,4},{6,5},{7,6},{9,8},{10,9},{11,10},{13,12},{... | collective-permute-start | bytes 98312 | tf_op jit(solution)/shard_map/ppermute | solution.py:12
  228.6 76.1 %copy-start.9 = (f32[256,8]{1,0:T(8,128)S(1)}, f32[256,8]{1,0:T(8,128)}, u32[]{:S(2)}) copy-start(f32[256,8]{1,0:T(8,128)} %copy-done.7) | copy-start | bytes 24580
  233.8 71.8 %copy-start.3 = (f32[896,128]{1,0:T(8,128)S(1)}, f32[896,128]{1,0:T(8,128)}, u32[]{:S(2)}) copy-start(f32[896,128]{1,0:T(8,128)} %get-tuple-element.17) | copy-start | bytes 1376260
  348.8 12.3 %copy-start.17 = (bf16[1,1,4,128,128]{4,3,2,1,0:T(8,128)(2,1)S(1)}, bf16[1,1,4,128,128]{4,3,2,1,0:T(8,128)(2,1)}, u32[]{:S(2)}) copy-start(bf16[1,1,4,128,128]{4,3,2,1,0:T(8,128)(2,1)} %param.15) | copy-start | bytes 393220
  349.7 8.3 %collective-permute-start.8 = (bf16[128,128]{1,0:T(8,128)(2,1)S(1)}, bf16[128,128]{1,0:T(8,128)(2,1)S(1)}, u32[]{:S(2)}, u32[]{:S(2)}) collective-permute-start(bf16[128,128]{1,0:T(8,128)(2,1)S(1)} %get-tuple-element.22), channel_id=1, source_target_pairs={{0,4},{4,8},{8,12},{12,16},{16,20},{20,24},{24,28},{1,5},{5,9},{9,... | collective-permute-start | bytes 98312 | tf_op jit(solution)/shard_map/ppermute | solution.py:12
  351.0 7.0 %collective-permute-start.10 = (bf16[128,128]{1,0:T(8,128)(2,1)S(1)}, bf16[128,128]{1,0:T(8,128)(2,1)S(1)}, u32[]{:S(2)}, u32[]{:S(2)}) collective-permute-start(bf16[128,128]{1,0:T(8,128)(2,1)S(1)} %get-tuple-element.23), channel_id=1, source_target_pairs={{0,1},{1,2},{2,3},{4,5},{5,6},{6,7},{8,9},{9,10},{10,11},{12,13},{... | collective-permute-start | bytes 98312 | tf_op jit(solution)/shard_map/ppermute | solution.py:12
  354.1 5.3 %collective-permute-start.9 = (bf16[128,128]{1,0:T(8,128)(2,1)S(1)}, bf16[128,128]{1,0:T(8,128)(2,1)S(1)}, u32[]{:S(2)}, u32[]{:S(2)}) collective-permute-start(bf16[128,128]{1,0:T(8,128)(2,1)S(1)} %get-tuple-element.24), channel_id=1, source_target_pairs={{4,0},{8,4},{12,8},{16,12},{20,16},{24,20},{28,24},{5,1},{9,5},{13... | collective-permute-start | bytes 98312 | tf_op jit(solution)/shard_map/ppermute | solution.py:12
  355.4 5.8 %collective-permute-start.11 = (bf16[128,128]{1,0:T(8,128)(2,1)S(1)}, bf16[128,128]{1,0:T(8,128)(2,1)S(1)}, u32[]{:S(2)}, u32[]{:S(2)}) collective-permute-start(bf16[128,128]{1,0:T(8,128)(2,1)S(1)} %get-tuple-element.25), channel_id=1, source_target_pairs={{1,0},{2,1},{3,2},{5,4},{6,5},{7,6},{9,8},{10,9},{11,10},{13,12},{... | collective-permute-start | bytes 98312 | tf_op jit(solution)/shard_map/ppermute | solution.py:12
  362.1 74.9 %copy-start.10 = (f32[256,8]{1,0:T(8,128)S(1)}, f32[256,8]{1,0:T(8,128)}, u32[]{:S(2)}) copy-start(f32[256,8]{1,0:T(8,128)} %copy-done.7) | copy-start | bytes 24580
  367.3 70.6 %copy-start.4 = (f32[896,128]{1,0:T(8,128)S(1)}, f32[896,128]{1,0:T(8,128)}, u32[]{:S(2)}) copy-start(f32[896,128]{1,0:T(8,128)} %get-tuple-element.17) | copy-start | bytes 1376260
  367.3 70.6 %copy-start.5 = (f32[896,128]{1,0:T(8,128)S(1)}, f32[896,128]{1,0:T(8,128)}, u32[]{:S(2)}) copy-start(f32[896,128]{1,0:T(8,128)} %get-tuple-element.37) | copy-start | bytes 1376260
  482.4 11.6 %copy-start.18 = (bf16[1,1,4,128,128]{4,3,2,1,0:T(8,128)(2,1)S(1)}, bf16[1,1,4,128,128]{4,3,2,1,0:T(8,128)(2,1)}, u32[]{:S(2)}) copy-start(bf16[1,1,4,128,128]{4,3,2,1,0:T(8,128)(2,1)} %param.15) | copy-start | bytes 393220
  483.3 7.6 %collective-permute-start.12 = (bf16[128,128]{1,0:T(8,128)(2,1)S(1)}, bf16[128,128]{1,0:T(8,128)(2,1)S(1)}, u32[]{:S(2)}, u32[]{:S(2)}) collective-permute-start(bf16[128,128]{1,0:T(8,128)(2,1)S(1)} %get-tuple-element.18), channel_id=1, source_target_pairs={{0,4},{4,8},{8,12},{12,16},{16,20},{20,24},{24,28},{1,5},{5,9},{9,... | collective-permute-start | bytes 98312 | tf_op jit(solution)/shard_map/ppermute | solution.py:12
  484.6 6.3 %collective-permute-start.14 = (bf16[128,128]{1,0:T(8,128)(2,1)S(1)}, bf16[128,128]{1,0:T(8,128)(2,1)S(1)}, u32[]{:S(2)}, u32[]{:S(2)}) collective-permute-start(bf16[128,128]{1,0:T(8,128)(2,1)S(1)} %get-tuple-element.19), channel_id=1, source_target_pairs={{0,1},{1,2},{2,3},{4,5},{5,6},{6,7},{8,9},{9,10},{10,11},{12,13},{... | collective-permute-start | bytes 98312 | tf_op jit(solution)/shard_map/ppermute | solution.py:12
  486.9 5.3 %collective-permute-start.13 = (bf16[128,128]{1,0:T(8,128)(2,1)S(1)}, bf16[128,128]{1,0:T(8,128)(2,1)S(1)}, u32[]{:S(2)}, u32[]{:S(2)}) collective-permute-start(bf16[128,128]{1,0:T(8,128)(2,1)S(1)} %get-tuple-element.20), channel_id=1, source_target_pairs={{4,0},{8,4},{12,8},{16,12},{20,16},{24,20},{28,24},{5,1},{9,5},{13... | collective-permute-start | bytes 98312 | tf_op jit(solution)/shard_map/ppermute | solution.py:12
  488.2 5.8 %collective-permute-start.15 = (bf16[128,128]{1,0:T(8,128)(2,1)S(1)}, bf16[128,128]{1,0:T(8,128)(2,1)S(1)}, u32[]{:S(2)}, u32[]{:S(2)}) collective-permute-start(bf16[128,128]{1,0:T(8,128)(2,1)S(1)} %get-tuple-element.21), channel_id=1, source_target_pairs={{1,0},{2,1},{3,2},{5,4},{6,5},{7,6},{9,8},{10,9},{11,10},{13,12},{... | collective-permute-start | bytes 98312 | tf_op jit(solution)/shard_map/ppermute | solution.py:12
  (3 other events, 9.2 us)
where the time goes:
time: 503 us; the launch traced here: 499 us
  blocking collectives  393 us (78%)
  other arithmetic  31.5 us (6%)
  starting transfers between devices  25.2 us (5%)
  matrix products  21.6 us (4%)
  local copies, waits for them, and re-layouts  13.2 us (3%)
  waiting for transfers between devices  12.8 us (3%)
    all_gather x4, blocking collectives, apply_prec(): stacked = lax.all_gather(coarse, ('gx', 'gy'), axis=0, tiled=True)  274 us
    psum x3, blocking collectives, shards(): lax.psum((jnp.sum(mapped * direction, axis=0), jnp.sum(mapped * mapped, a...  119 us
    ppermute x16, starting transfers between devices, from_behind(): lax.ppermute(value, axis, [(source, source + steps) for source in range(l...  25.2 us
    scatter-add x4, other arithmetic, apply_schur(): return result.at[flat_rows].add(-coupled.reshape(-1, coupled.shape[-1]))  19.1 us
    ppermute x16, waiting for transfers between devices, from_behind(): lax.ppermute(value, axis, [(source, source + steps) for source in range(l...  12.8 us
  transfers between devices with their start and end apart: 16, of which 7 were waited for; matrix products, arithmetic and copies ran while one was open for 1% of the time, Pallas kernels for 0%

commit v1 on v0

--- a/solution.py
+++ b/solution.py
@@ -1,6 +1,10 @@
+import functools
+
 import jax
 import jax.numpy as jnp
 from jax import lax
+from jax.experimental import pallas as pl
+from jax.experimental.pallas import tpu as pltpu
 from jax.sharding import PartitionSpec as P
 
 ITERS = 3
@@ -88,9 +92,392 @@
     return (solution[None, None], residual[None, None])
 
 
+MESH = pl.DeviceIdType.MESH
+REPLICATED_COARSE = 512
+
+
+def wide_dot(left, right):
+    return jnp.dot(left, right, precision=lax.Precision.HIGHEST, preferred_element_type=jnp.float32)
+
+
+def dot16(left, right):
+    return jnp.dot(left, right, preferred_element_type=jnp.float32)
+
+
+def pieces(value):
+    high = value.astype(jnp.bfloat16)
+    rest = value - high.astype(jnp.float32)
+    middle = rest.astype(jnp.bfloat16)
+    low = (rest - middle.astype(jnp.float32)).astype(jnp.bfloat16)
+    return high, middle, low
+
+
+def exact_dot(left, value):
+    cols = value.shape[1]
+    out = dot16(left, jnp.concatenate(pieces(value), axis=1))
+    return out[:, :cols] + (out[:, cols : 2 * cols] + out[:, 2 * cols :])
+
+
+def kernel(
+    gx,
+    gy,
+    rhs_ref,
+    schur_ref,
+    sdiag_ref,
+    trace_ref,
+    tdiag_ref,
+    coup_ref,
+    rows_ref,
+    defl_ref,
+    cinv_ref,
+    cmap_ref,
+    x_ref,
+    res_ref,
+    sb_ref,
+    pick_ref,
+    v_ref,
+    sd_ref,
+    td_ref,
+    d_ref,
+    dh_ref,
+    xh_ref,
+    e_ref,
+    solved_ref,
+    dt_ref,
+    dht_ref,
+    cp_ref,
+    gram_ref,
+    a_buf,
+    b_buf,
+    extra,
+    halo,
+    halo_d,
+    halo_d_out,
+    halo_out,
+    a_send,
+    a_recv,
+    b_send,
+    b_recv,
+    ea_send,
+    ea_recv,
+    eb_send,
+    eb_recv,
+    h_send,
+    h_recv,
+    hd_send,
+    hd_recv,
+):
+    f32, bf16 = jnp.float32, jnp.bfloat16
+    rows, src = rhs_ref.shape
+    ov = rows_ref.shape[1]
+    k = defl_ref.shape[0]
+    nc = cinv_ref.shape[1]
+    me_x, me_y = lax.axis_index("gx"), lax.axis_index("gy")
+    place = me_x * gy + me_y
+    iters = ITERS
+
+    along_x = [lax.rem(me_x + step, gx) for step in range(1, gx)]
+    along_y = [lax.rem(me_y + step, gy) for step in range(1, gy)]
+    near = [
+        (me_x > 0, (jnp.maximum(me_x - 1, 0), me_y)),
+        (me_x < gx - 1, (jnp.minimum(me_x + 1, gx - 1), me_y)),
+        (me_y > 0, (me_x, jnp.maximum(me_y - 1, 0))),
+        (me_y < gy - 1, (me_x, jnp.minimum(me_y + 1, gy - 1))),
+    ]
+
+    halo[...] = jnp.zeros_like(halo)
+    halo_d[...] = jnp.zeros_like(halo_d)
+
+    barrier = pltpu.get_barrier_semaphore()
+    for other in along_x:
+        pl.semaphore_signal(barrier, inc=1, device_id=(other, me_y), device_id_type=MESH)
+    for other in along_y:
+        pl.semaphore_signal(barrier, inc=1, device_id=(me_x, other), device_id_type=MESH)
+
+    def remote(source, target, send, recv, device):
+        return pltpu.make_async_remote_copy(
+            src_ref=source, dst_ref=target, send_sem=send, recv_sem=recv, device_id=device, device_id_type=MESH
+        )
+
+    defl = defl_ref[...]
+    defl_wide = defl.astype(f32)
+    tiled = jnp.concatenate([defl_wide] * (nc // k), axis=0).astype(bf16)
+    gram = lax.dot_general(defl, tiled, (((1,), (1,)), ((), ())), preferred_element_type=f32)
+    column = lax.broadcasted_iota(jnp.int32, (k, nc), 1)
+    own = (column >= place * k) & (column < place * k + k)
+    extra[me_x, me_y, 0:k, :] = cinv_ref[...]
+    extra[me_x, me_y, k : 2 * k, :] = jnp.where(own, gram, 0.0)
+
+    pl.semaphore_wait(barrier, gx + gy - 2)
+
+    extra_a = [
+        remote(extra.at[me_x, me_y], extra.at[me_x, me_y], ea_send.at[i], ea_recv.at[i], (me_x, other))
+        for i, other in enumerate(along_y)
+    ]
+    for copy in extra_a:
+        copy.start()
+
+    def column_of(ref):
+        return jnp.transpose(jnp.broadcast_to(ref[...], (src, rows)))
+
+    td_ref[...] = column_of(tdiag_ref)
+    sd_ref[...] = column_of(sdiag_ref)
+
+    def local_prec(rounded):
+        q = td_ref[...] * rounded.astype(f32) + dot16(trace_ref[...], rounded)
+        return q, dot16(defl, rounded)
+
+    def start_sums(t, q, coarse, sums):
+        a_buf[t, me_y, 0:k, :] = coarse
+        a_buf[t, me_y, k : 2 * k, :] = exact_dot(defl, q)
+        a_buf[t, me_y, 2 * k : 3 * k, :] = sums
+
+    def a_copies(t):
+        return [
+            remote(a_buf.at[t, me_y], a_buf.at[t, me_y], a_send.at[t, i], a_recv.at[t, i], (me_x, other))
+            for i, other in enumerate(along_y)
+        ]
+
+    def b_copies(t):
+        return [
+            remote(b_buf.at[t, me_x], b_buf.at[t, me_x], b_send.at[t, i], b_recv.at[t, i], (other, me_y))
+            for i, other in enumerate(along_x)
+        ]
+
+    def halo_copies(t):
+        return [
+            remote(halo_out.at[t, d], halo.at[t, d ^ 1], h_send.at[t, d], h_recv.at[t, d ^ 1], near[d][1])
+            for d in range(4)
+        ]
+
+    def halo_waits(t):
+        return [
+            remote(halo_out.at[t, d], halo.at[t, d], h_send.at[t, d], h_recv.at[t, d], near[d][1])
+            for d in range(4)
+        ]
+
+    def exchange(t, q, coarse, sums, with_halo):
+        start_sums(t, q, coarse, sums)
+        first = a_copies(t)
+        for copy in first:
+            copy.start()
+
+        def send_halo():
+            picked = exact_dot(pick_ref[...], q)
+            for d in range(4):
+                halo_out[t, d, :, :] = picked[d * ov : (d + 1) * ov]
+            for d, copy in enumerate(halo_copies(t)):
+                pl.when(near[d][0])(copy.start)
+
+        if with_halo is True:
+            send_halo()
+        else:
+            pl.when(with_halo)(send_halo)
+        for copy in first:
+            copy.wait()
+        total = jnp.zeros((k, src), f32)
+        for b in range(gy):
+            b_buf[t, me_x, b * k : (b + 1) * k, :] = a_buf[t, b, 0:k, :]
+            b_buf[t, me_x, (gy + b) * k : (gy + b + 1) * k, :] = a_buf[t, b, k : 2 * k, :]
+            total = total + a_buf[t, b, 2 * k : 3 * k, :]
+        b_buf[t, me_x, 2 * gy * k :, :] = total
+        second = b_copies(t)
+        for copy in second:
+            copy.start()
+        return second
+
+    def gathered(t):
+        coarse_all = jnp.concatenate([b_buf[t, a, 0 : gy * k, :] for a in range(gx)], axis=0)
+        dq_all = jnp.concatenate([b_buf[t, a, gy * k : 2 * gy * k, :] for a in range(gx)], axis=0)
+        total = b_buf[t, 0, 2 * gy * k :, :]
+        for a in range(1, gx):
+            total = total + b_buf[t, a, 2 * gy * k :, :]
+        return coarse_all, dq_all, total
+
+    def solve(coarse_all, dq_all):
+        solved = wide_dot(cp_ref[...], coarse_all)
+        solved_ref[...] = solved
+        return solved, dq_all + wide_dot(gram_ref[...], solved)
+
+    def solved_of(device):
+        at = (device[0] * gy + device[1]) * k
+        return jnp.concatenate(pieces(solved_ref[pl.ds(pl.multiple_of(at, k), k), :]), axis=0)
+
+    def halo_mapped(t):
+        for d, copy in enumerate(halo_waits(t)):
+            pl.when(near[d][0])(copy.wait)
+        return [
+            halo[t, d, :, :] + dot16(dht_ref[d, :, :], solved_of(near[d][1])) for d in range(4)
+        ]
+
+    for d in range(4):
+        wanted = jnp.transpose(jnp.broadcast_to(rows_ref[d : d + 1, :].astype(f32), (ov, ov)))
+        wanted = jnp.concatenate([wanted] * (rows // ov), axis=1).astype(jnp.int32)
+        hot = wanted == lax.broadcasted_iota(jnp.int32, (ov, rows), 1)
+        pick_ref[d * ov : (d + 1) * ov, :] = jnp.where(hot, 1.0, 0.0).astype(bf16)
+
+    q0, coarse0 = local_prec(rhs_ref[...])
+    pending = exchange(0, q0, coarse0, jnp.zeros((k, src), f32), True)
+    for copy in extra_a:
+        copy.wait()
+    extra_b = [
+        remote(extra.at[me_x], extra.at[me_x], eb_send.at[i], eb_recv.at[i], (other, me_y))
+        for i, other in enumerate(along_x)
+    ]
+    for copy in extra_b:
+        copy.start()
+
+    for d in range(4):
+        halo_d_out[d, :, :] = lax.dot_general(
+            defl, pick_ref[d * ov : (d + 1) * ov, :], (((1,), (1,)), ((), ())), preferred_element_type=f32
+        )
+        copy = remote(halo_d_out.at[d], halo_d.at[d ^ 1], hd_send.at[d], hd_recv.at[d ^ 1], near[d][1])
+        pl.when(near[d][0])(copy.start)
+
+    sb_ref[:, 0:rows] = schur_ref[...]
+    for d in range(4):
+        hot = rows_ref[d : d + 1, :] == lax.broadcasted_iota(jnp.int32, (rows, ov), 0)
+        spread = dot16(jnp.where(hot, -1.0, 0.0).astype(bf16), coup_ref[d, :, :])
+        sb_ref[:, rows + d * ov : rows + (d + 1) * ov] = spread.astype(bf16)
+    dt_ref[...] = jnp.transpose(jnp.concatenate([defl_wide] * 3, axis=0)).astype(bf16)
+    for d in range(4):
+        arrival = remote(halo_d_out.at[d], halo_d.at[d], hd_send.at[d], hd_recv.at[d], near[d][1])
+        pl.when(near[d][0])(arrival.wait)
+        dht_ref[d, :, :] = jnp.transpose(jnp.concatenate([halo_d[d, :, :]] * 3, axis=0)).astype(bf16)
+
+    for copy in extra_b:
+        copy.wait()
+    inverse = jnp.concatenate([extra[a, b, 0:k, :] for a in range(gx) for b in range(gy)], axis=0)
+    gram_ref[...] = jnp.concatenate([extra[a, b, k : 2 * k, :] for a in range(gx) for b in range(gy)], axis=0)
+    order = cmap_ref[...] == lax.broadcasted_iota(jnp.int32, (nc, nc), 0)
+    cp_ref[...] = wide_dot(inverse, jnp.where(order, 1.0, 0.0))
+
+    for copy in pending:
+        copy.wait()
+    coarse_all, dq_all, _ = gathered(0)
+    solved, projected = solve(coarse_all, dq_all)
+    e_ref[...] = projected
+    d_ref[...] = q0 + dot16(dt_ref[...], solved_of((me_x, me_y)))
+    dh_ref[...] = jnp.concatenate(halo_mapped(0), axis=0)
+    x_ref[...] = jnp.zeros_like(x_ref)
+    xh_ref[...] = jnp.zeros_like(xh_ref)
+
+    def schur(field_ref, margin_ref):
+        v_ref[0:rows, :] = field_ref[...].astype(bf16)
+        v_ref[rows:, :] = margin_ref[...].astype(bf16)
+        return sd_ref[...] * v_ref[0:rows, :].astype(f32) + dot16(sb_ref[...], v_ref[...])
+
+    def iteration(step, carry):
+        t = step + 1
+        more = t < iters
+        q, coarse = local_prec(schur(d_ref, dh_ref).astype(bf16))
+        sums = jnp.concatenate(
+            [
+                jnp.sum(q * d_ref[...], axis=0, keepdims=True),
+                jnp.sum(q * q, axis=0, keepdims=True),
+                jnp.zeros((k - 2, src), f32),
+            ],
+            axis=0,
+        )
+        for copy in exchange(t, q, coarse, sums, more):
+            copy.wait()
+        coarse_all, dq_all, total = gathered(t)
+        solved, projected = solve(coarse_all, dq_all)
+        numer = total[0:1] + jnp.sum(solved * e_ref[...], axis=0, keepdims=True)
+        denom = total[1:2] + jnp.sum(solved * (dq_all + projected), axis=0, keepdims=True)
+        alpha = numer / denom
+        x_ref[...] += alpha * d_ref[...]
+        xh_ref[...] += alpha * dh_ref[...]
+
+        @pl.when(more)
+        def _():
+            d_ref[...] -= alpha * (q + dot16(dt_ref[...], solved_of((me_x, me_y))))
+            e_ref[...] -= alpha * projected
+            dh_ref[...] -= alpha * jnp.concatenate(halo_mapped(t), axis=0)
+
+        return carry
+
+    lax.fori_loop(0, iters, iteration, 0)
+    res_ref[...] = rhs_ref[...].astype(f32) - schur(x_ref, xh_ref)
+
+
+def one_kernel(gx, gy, *args):
+    right_side, schur, sdiag, trace, tdiag, couplings, margin, deflation, inverse, coarse_map = args
+    rows, src = right_side.shape[2:]
+    ov = margin.shape[3]
+    k = deflation.shape[2]
+    nc = inverse.shape[1]
+    f32, bf16 = jnp.float32, jnp.bfloat16
+    rounds = ITERS + 1
+    vmem, dma = pltpu.VMEM, pltpu.SemaphoreType.DMA
+    x, residual = pl.pallas_call(
+        functools.partial(kernel, gx, gy),
+        out_shape=[jax.ShapeDtypeStruct((rows, src), f32)] * 2,
+        in_specs=[pl.BlockSpec(memory_space=pltpu.VMEM)] * 10,
+        out_specs=[pl.BlockSpec(memory_space=pltpu.VMEM)] * 2,
+        scratch_shapes=[
+            vmem((rows, rows + 4 * ov), bf16),
+            vmem((4 * ov, rows), bf16),
+            vmem((rows + 4 * ov, src), bf16),
+            vmem((rows, src), f32),
+            vmem((rows, src), f32),
+            vmem((rows, src), f32),
+            vmem((4 * ov, src), f32),
+            vmem((4 * ov, src), f32),
+            vmem((nc, src), f32),
+            vmem((nc, src), f32),
+            vmem((rows, 3 * k), bf16),
+            vmem((4, ov, 3 * k), bf16),
+            vmem((nc, nc), f32),
+            vmem((nc, nc), f32),
+            vmem((rounds, gy, 3 * k, src), f32),
+            vmem((rounds, gx, (2 * gy + 1) * k, src), f32),
+            vmem((gx, gy, 2 * k, nc), f32),
+            vmem((rounds, 4, ov, src), f32),
+            vmem((4, k, ov), f32),
+            vmem((4, k, ov), f32),
+            vmem((rounds, 4, ov, src), f32),
+            dma((rounds, gy - 1)),
+            dma((rounds, gy - 1)),
+            dma((rounds, gx - 1)),
+            dma((rounds, gx - 1)),
+            dma((gy - 1,)),
+            dma((gy - 1,)),
+            dma((gx - 1,)),
+            dma((gx - 1,)),
+            dma((rounds, 4)),
+            dma((rounds, 4)),
+            dma((4,)),
+            dma((4,)),
+        ],
+        compiler_params=pltpu.CompilerParams(
+            collective_id=0, has_side_effects=True, vmem_limit_bytes=48 * 1024 * 1024
+        ),
+        cost_estimate=pl.CostEstimate(flops=4_000_000_000, bytes_accessed=6_000_000, transcendentals=0),
+    )(
+        right_side[0, 0],
+        schur[0, 0],
+        sdiag[0],
+        trace[0, 0],
+        tdiag[0],
+        couplings[0, 0],
+        margin[0, 0],
+        deflation[0, 0],
+        inverse,
+        coarse_map[None],
+    )
+    return x[None, None], residual[None, None]
+
+
+def plan(gx, gy, *args):
+    if args[8].shape[1] <= REPLICATED_COARSE:
+        return one_kernel(gx, gy, *args)
+    return shards(*args)
+
+
 def solution(mesh):
     return jax.shard_map(
-        shards,
+        functools.partial(plan, mesh.shape["gx"], mesh.shape["gy"]),
         mesh=mesh,
         in_specs=(
             P("gx", "gy", None, None),

time: 503 us -> 71.7 us (0.14)
  blocking collectives: 393 us -> 0 us
  Pallas kernels: 0 us -> 60.3 us
  other arithmetic: 31.5 us -> 0 us
  starting transfers between devices: 25.2 us -> 0 us
  matrix products: 21.6 us -> 0 us
  waiting for transfers between devices: 12.8 us -> 0 us
    all_gather x4 -> x0, blocking collectives: 274 us -> none  [apply_prec(): stacked = lax.all_gather(coarse, ('gx', 'gy'), axis=0, tiled=True)]
    psum x3 -> x0, blocking collectives: 119 us -> none  [shards(): lax.psum((jnp.sum(mapped * direction, axis=0), jnp.sum(mapped * mapped, a...]
    pallas_call x0 -> x1, Pallas kernels: none -> 60.3 us  [one_kernel(): pl.pallas_call(functools.partial(kernel, gx, gy), out_shape=[jax.ShapeDty...]
    ppermute x16 -> x0, starting transfers between devices: 25.2 us -> none  [from_behind(): lax.ppermute(value, axis, [(source, source + steps) for source in range(l...]
    dot_general x24 -> x0, matrix products: 21.6 us -> none  [the longest x4 6.06 us: apply_prec(): jnp.dot(trace_mat, rounded, preferred_element_type=jnp.float32)]
    scatter-add x4 -> x0, other arithmetic: 19.1 us -> none  [apply_schur(): return result.at[flat_rows].add(-coupled.reshape(-1, coupled.shape[-1]))]
    ppermute x16 -> x0, waiting for transfers between devices: 12.8 us -> none  [from_behind(): lax.ppermute(value, axis, [(source, source + steps) for source in range(l...]
    unnamed x39 -> x22, local copies, waits for them, and re-layouts: 0.9 us -> 10.3 us
  transfers between devices with their start and end apart: 16 -> 0, of which waited for: 7 -> 0; matrix products, arithmetic and copies ran while one was open for 1% -> 0% of each run, Pallas kernels for 0% -> 0%
where the time goes in v1:
time: 71.7 us; the launch traced here: 71.3 us
  Pallas kernels  60.3 us (84%)
  local copies, waits for them, and re-layouts  10.3 us (14%)
    pallas_call x1, Pallas kernels, one_kernel(): pl.pallas_call(functools.partial(kernel, gx, gy), out_shape=[jax.ShapeDty...  60.3 us
    unnamed x22, local copies, waits for them, and re-layouts  10.3 us

profile of v1, /device:TPU:0, one launch (start us, length us, event | category | flops | bytes accessed | tf_op | source)
XLA Modules:
  0.0 71.3 jit_solution(1287448996854127361)
XLA Ops:
  0.6 0.0 copy-start
  0.6 1.4 %copy-done = bf16[1,1,896,896]{3,2,1,0:T(8,128)(2,1)S(1)} copy-done((bf16[1,1,896,896]{3,2,1,0:T(8,128)(2,1)S(1)}, bf16[1,1,896,896]{3,2,1,0:T(8,128)(2,1)}, u32[]{:S(2)}) %copy-start) | copy-done | bytes 1605656
  2.1 0.0 copy-start.1
  2.1 1.4 %copy-done.1 = bf16[1,1,896,896]{3,2,1,0:T(8,128)(2,1)S(1)} copy-done((bf16[1,1,896,896]{3,2,1,0:T(8,128)(2,1)S(1)}, bf16[1,1,896,896]{3,2,1,0:T(8,128)(2,1)}, u32[]{:S(2)}) %copy-start.1) | copy-done | bytes 1605656
  3.5 0.0 copy-start.2
  3.5 0.9 %copy-done.2 = bf16[1,1,896,128]{3,2,1,0:T(8,128)(2,1)S(1)} copy-done((bf16[1,1,896,128]{3,2,1,0:T(8,128)(2,1)S(1)}, bf16[1,1,896,128]{3,2,1,0:T(8,128)(2,1)}, u32[]{:S(2)}) %copy-start.2) | copy-done | bytes 229400
  4.4 0.0 copy-start.3
  4.4 0.9 %copy-done.3 = bf16[1,1,4,128,128]{4,3,2,1,0:T(8,128)(2,1)S(1)} copy-done((bf16[1,1,4,128,128]{4,3,2,1,0:T(8,128)(2,1)S(1)}, bf16[1,1,4,128,128]{4,3,2,1,0:T(8,128)(2,1)}, u32[]{:S(2)}) %copy-start.3) | copy-done | bytes 131096
  5.3 0.0 copy-start.4
  5.3 0.7 copy-done.4
  6.0 0.0 copy-start.5
  6.0 0.7 copy-done.5
  6.7 0.0 copy-start.6
  6.7 0.7 copy-done.6
  7.4 0.0 copy-start.7
  7.4 0.7 copy-done.7
  8.1 0.0 copy-start.8
  8.1 0.7 copy-done.8
  8.8 0.0 copy-start.9
  8.8 0.7 copy-done.9
  9.5 60.3 %shard_map.113 = (f32[896,128]{1,0:T(8,128)S(1)}, f32[896,128]{1,0:T(8,128)S(1)}) custom-call(bf16[896,128]{1,0:T(8,128)(2,1)S(1)} %bitcast.15, bf16[896,896]{1,0:T(8,128)(2,1)S(1)} %bitcast.13, f32[1,896]{1,0:T(1,128)S(1)} %bitcast.18, bf16[896,896]{1,0:T(8,128)(2,1)S(1)} %bitcast.14, f32[1,896]{1,0:T(1,128)S(1)} %bitcast.19, ...), custom_call_target="tpu_custom_call" | custom-call | flops 4000000000 | bytes 6000000 | tf_op jit(solution)/shard_map/pallas_call | solution.py:413
  69.8 0.8 %copy.14 = f32[1,1,896,128]{3,2,1,0:T(8,128)} copy(f32[1,1,896,128]{3,2,1,0:T(8,128)S(1)} %bitcast.12) | data formatting | bytes 917504
  70.5 0.8 %copy.15 = f32[1,1,896,128]{3,2,1,0:T(8,128)} copy(f32[1,1,896,128]{3,2,1,0:T(8,128)S(1)} %bitcast.11) | data formatting | bytes 917504
Async XLA Ops:
  0.6 1.4 %copy-start = (bf16[1,1,896,896]{3,2,1,0:T(8,128)(2,1)S(1)}, bf16[1,1,896,896]{3,2,1,0:T(8,128)(2,1)}, u32[]{:S(2)}) copy-start(bf16[1,1,896,896]{3,2,1,0:T(8,128)(2,1)} %param.11) | copy-start | bytes 4816900
  2.1 1.4 %copy-start.1 = (bf16[1,1,896,896]{3,2,1,0:T(8,128)(2,1)S(1)}, bf16[1,1,896,896]{3,2,1,0:T(8,128)(2,1)}, u32[]{:S(2)}) copy-start(bf16[1,1,896,896]{3,2,1,0:T(8,128)(2,1)} %param.13) | copy-start | bytes 4816900
  3.5 0.9 %copy-start.2 = (bf16[1,1,896,128]{3,2,1,0:T(8,128)(2,1)S(1)}, bf16[1,1,896,128]{3,2,1,0:T(8,128)(2,1)}, u32[]{:S(2)}) copy-start(bf16[1,1,896,128]{3,2,1,0:T(8,128)(2,1)} %param.10) | copy-start | bytes 688132
  4.4 0.9 %copy-start.3 = (bf16[1,1,4,128,128]{4,3,2,1,0:T(8,128)(2,1)S(1)}, bf16[1,1,4,128,128]{4,3,2,1,0:T(8,128)(2,1)}, u32[]{:S(2)}) copy-start(bf16[1,1,4,128,128]{4,3,2,1,0:T(8,128)(2,1)} %param.15) | copy-start | bytes 393220
  5.3 0.7 copy-start.4
  6.0 0.7 copy-start.5
  6.7 0.7 copy-start.6
  7.4 0.7 copy-start.7
  8.1 0.7 copy-start.8
  8.8 0.7 copy-start.9

commit v2 on v1

--- a/solution.py
+++ b/solution.py
@@ -118,21 +118,37 @@
     return out[:, :cols] + (out[:, cols : 2 * cols] + out[:, 2 * cols :])
 
 
+def six(value, left):
+    high, middle, low = pieces(value)
+    if left:
+        return jnp.concatenate([high, high, high, middle, middle, low], axis=1)
+    return jnp.concatenate([high, middle, low, high, middle, high], axis=0)
+
+
 def kernel(
     gx,
     gy,
+    rhs_hbm,
+    schur_hbm,
+    sdiag_hbm,
+    trace_hbm,
+    tdiag_hbm,
+    coup_hbm,
+    rows_hbm,
+    defl_hbm,
+    cinv_hbm,
+    cmap_hbm,
+    x_ref,
+    res_ref,
     rhs_ref,
-    schur_ref,
     sdiag_ref,
     trace_ref,
     tdiag_ref,
     coup_ref,
     rows_ref,
     defl_ref,
-    cinv_ref,
     cmap_ref,
-    x_ref,
-    res_ref,
+    load_sem,
     sb_ref,
     pick_ref,
     v_ref,
@@ -145,10 +161,11 @@
     solved_ref,
     dt_ref,
     dht_ref,
-    cp_ref,
-    gram_ref,
-    a_buf,
-    b_buf,
+    both_ref,
+    small_ref,
+    main,
+    sum_a,
+    sum_b,
     extra,
     halo,
     halo_d,
@@ -158,6 +175,10 @@
     a_recv,
     b_send,
     b_recv,
+    sa_send,
+    sa_recv,
+    sb_send,
+    sb_recv,
     ea_send,
     ea_recv,
     eb_send,
@@ -171,10 +192,25 @@
     rows, src = rhs_ref.shape
     ov = rows_ref.shape[1]
     k = defl_ref.shape[0]
-    nc = cinv_ref.shape[1]
+    nc = cmap_ref.shape[1]
     me_x, me_y = lax.axis_index("gx"), lax.axis_index("gy")
-    place = me_x * gy + me_y
     iters = ITERS
+
+    def load(i, source, target):
+        copy = pltpu.make_async_copy(source, target, load_sem.at[i])
+        copy.start()
+        return copy
+
+    load_defl = load(0, defl_hbm, defl_ref)
+    load_cinv = load(1, cinv_hbm, extra.at[me_x, me_y, :, pl.ds(0, nc)])
+    load_tdiag = load(2, tdiag_hbm, tdiag_ref)
+    load_rhs = load(3, rhs_hbm, rhs_ref)
+    load_trace = load(4, trace_hbm, trace_ref)
+    load_rows = load(5, rows_hbm, rows_ref)
+    load_cmap = load(6, cmap_hbm, cmap_ref)
+    load_sdiag = load(7, sdiag_hbm, sdiag_ref)
+    load_coup = load(8, coup_hbm, coup_ref)
+    load_schur = load(9, schur_hbm, sb_ref.at[:, pl.ds(0, rows)])
 
     along_x = [lax.rem(me_x + step, gx) for step in range(1, gx)]
     along_y = [lax.rem(me_y + step, gy) for step in range(1, gy)]
@@ -185,8 +221,12 @@
         (me_y < gy - 1, (me_x, jnp.minimum(me_y + 1, gy - 1))),
     ]
 
-    halo[...] = jnp.zeros_like(halo)
-    halo_d[...] = jnp.zeros_like(halo_d)
+    for d in range(4):
+
+        @pl.when(jnp.logical_not(near[d][0]))
+        def _():
+            halo[:, d, :, :] = jnp.zeros((iters, ov, src), f32)
+            halo_d[d, :, :] = jnp.zeros((k, ov), f32)
 
     barrier = pltpu.get_barrier_semaphore()
     for other in along_x:
@@ -199,134 +239,107 @@
             src_ref=source, dst_ref=target, send_sem=send, recv_sem=recv, device_id=device, device_id_type=MESH
         )
 
+    def to_lines(ref, send, recv):
+        return [remote(ref, ref, send.at[i], recv.at[i], (me_x, other)) for i, other in enumerate(along_y)]
+
+    def to_columns(ref, send, recv):
+        return [remote(ref, ref, send.at[i], recv.at[i], (other, me_y)) for i, other in enumerate(along_x)]
+
+    def start(copies):
+        for copy in copies:
+            copy.start()
+
+    def wait(copies):
+        for copy in copies:
+            copy.wait()
+
+    load_defl.wait()
     defl = defl_ref[...]
     defl_wide = defl.astype(f32)
-    tiled = jnp.concatenate([defl_wide] * (nc // k), axis=0).astype(bf16)
-    gram = lax.dot_general(defl, tiled, (((1,), (1,)), ((), ())), preferred_element_type=f32)
-    column = lax.broadcasted_iota(jnp.int32, (k, nc), 1)
-    own = (column >= place * k) & (column < place * k + k)
-    extra[me_x, me_y, 0:k, :] = cinv_ref[...]
-    extra[me_x, me_y, k : 2 * k, :] = jnp.where(own, gram, 0.0)
-
+    padded = jnp.concatenate([defl_wide, jnp.zeros((src - k, rows), f32)], axis=0).astype(bf16)
+    extra[me_x, me_y, :, nc:] = lax.dot_general(
+        defl, padded, (((1,), (1,)), ((), ())), preferred_element_type=f32
+    )
+    load_cinv.wait()
     pl.semaphore_wait(barrier, gx + gy - 2)
 
-    extra_a = [
-        remote(extra.at[me_x, me_y], extra.at[me_x, me_y], ea_send.at[i], ea_recv.at[i], (me_x, other))
-        for i, other in enumerate(along_y)
-    ]
-    for copy in extra_a:
-        copy.start()
-
-    def column_of(ref):
-        return jnp.transpose(jnp.broadcast_to(ref[...], (src, rows)))
-
-    td_ref[...] = column_of(tdiag_ref)
-    sd_ref[...] = column_of(sdiag_ref)
+    extra_a = to_lines(extra.at[me_x, me_y], ea_send, ea_recv)
+    start(extra_a)
+
+    load_tdiag.wait()
+    load_trace.wait()
+    with_trace = defl_wide * tdiag_ref[...] + dot16(defl, trace_ref[...])
+    small_ref[...] = jnp.concatenate(
+        [defl_wide] + [piece.astype(f32) for piece in pieces(with_trace)], axis=0
+    ).astype(bf16)
+
+    def coarse_copies(t):
+        return (
+            to_lines(main.at[t, me_x, me_y], a_send.at[t], a_recv.at[t]),
+            to_columns(main.at[t, me_x], b_send.at[t], b_recv.at[t]),
+        )
+
+    def start_coarse(t, rounded):
+        out = dot16(small_ref[...], rounded)
+        main[t, me_x, me_y, 0:k, :] = out[0:k]
+        main[t, me_x, me_y, k : 2 * k, :] = out[k : 2 * k] + (out[2 * k : 3 * k] + out[3 * k : 4 * k])
+        start(coarse_copies(t)[0])
+
+    def forward_coarse(t):
+        first, second = coarse_copies(t)
+        wait(first)
+        start(second)
 
     def local_prec(rounded):
-        q = td_ref[...] * rounded.astype(f32) + dot16(trace_ref[...], rounded)
-        return q, dot16(defl, rounded)
-
-    def start_sums(t, q, coarse, sums):
-        a_buf[t, me_y, 0:k, :] = coarse
-        a_buf[t, me_y, k : 2 * k, :] = exact_dot(defl, q)
-        a_buf[t, me_y, 2 * k : 3 * k, :] = sums
-
-    def a_copies(t):
+        return td_ref[...] * rounded.astype(f32) + dot16(trace_ref[...], rounded)
+
+    def halo_copies(t, arriving):
         return [
-            remote(a_buf.at[t, me_y], a_buf.at[t, me_y], a_send.at[t, i], a_recv.at[t, i], (me_x, other))
-            for i, other in enumerate(along_y)
-        ]
-
-    def b_copies(t):
-        return [
-            remote(b_buf.at[t, me_x], b_buf.at[t, me_x], b_send.at[t, i], b_recv.at[t, i], (other, me_y))
-            for i, other in enumerate(along_x)
-        ]
-
-    def halo_copies(t):
-        return [
-            remote(halo_out.at[t, d], halo.at[t, d ^ 1], h_send.at[t, d], h_recv.at[t, d ^ 1], near[d][1])
+            remote(
+                halo_out.at[t, d],
+                halo.at[t, d if arriving else d ^ 1],
+                h_send.at[t, d],
+                h_recv.at[t, d if arriving else d ^ 1],
+                near[d][1],
+            )
             for d in range(4)
         ]
 
-    def halo_waits(t):
-        return [
-            remote(halo_out.at[t, d], halo.at[t, d], h_send.at[t, d], h_recv.at[t, d], near[d][1])
-            for d in range(4)
-        ]
-
-    def exchange(t, q, coarse, sums, with_halo):
-        start_sums(t, q, coarse, sums)
-        first = a_copies(t)
-        for copy in first:
-            copy.start()
-
-        def send_halo():
-            picked = exact_dot(pick_ref[...], q)
-            for d in range(4):
-                halo_out[t, d, :, :] = picked[d * ov : (d + 1) * ov]
-            for d, copy in enumerate(halo_copies(t)):
-                pl.when(near[d][0])(copy.start)
-
-        if with_halo is True:
-            send_halo()
-        else:
-            pl.when(with_halo)(send_halo)
-        for copy in first:
-            copy.wait()
-        total = jnp.zeros((k, src), f32)
-        for b in range(gy):
-            b_buf[t, me_x, b * k : (b + 1) * k, :] = a_buf[t, b, 0:k, :]
-            b_buf[t, me_x, (gy + b) * k : (gy + b + 1) * k, :] = a_buf[t, b, k : 2 * k, :]
-            total = total + a_buf[t, b, 2 * k : 3 * k, :]
-        b_buf[t, me_x, 2 * gy * k :, :] = total
-        second = b_copies(t)
-        for copy in second:
-            copy.start()
-        return second
-
-    def gathered(t):
-        coarse_all = jnp.concatenate([b_buf[t, a, 0 : gy * k, :] for a in range(gx)], axis=0)
-        dq_all = jnp.concatenate([b_buf[t, a, gy * k : 2 * gy * k, :] for a in range(gx)], axis=0)
-        total = b_buf[t, 0, 2 * gy * k :, :]
-        for a in range(1, gx):
-            total = total + b_buf[t, a, 2 * gy * k :, :]
-        return coarse_all, dq_all, total
-
-    def solve(coarse_all, dq_all):
-        solved = wide_dot(cp_ref[...], coarse_all)
-        solved_ref[...] = solved
-        return solved, dq_all + wide_dot(gram_ref[...], solved)
+    def send_halo(t, q):
+        picked = exact_dot(pick_ref[...], q)
+        for d in range(4):
+            halo_out[t, d, :, :] = picked[d * ov : (d + 1) * ov]
+        for d, copy in enumerate(halo_copies(t, False)):
+            pl.when(near[d][0])(copy.start)
+
+    def solve(t):
+        wait(coarse_copies(t)[1])
+        coarse_all = jnp.concatenate([main[t, a, b, 0:k, :] for a in range(gx) for b in range(gy)], axis=0)
+        dq_all = jnp.concatenate([main[t, a, b, k : 2 * k, :] for a in range(gx) for b in range(gy)], axis=0)
+        both = dot16(both_ref[...], six(coarse_all, False))
+        solved_ref[...] = both[0:nc]
+        return both[0:nc], dq_all, dq_all + both[nc:]
 
     def solved_of(device):
         at = (device[0] * gy + device[1]) * k
         return jnp.concatenate(pieces(solved_ref[pl.ds(pl.multiple_of(at, k), k), :]), axis=0)
 
     def halo_mapped(t):
-        for d, copy in enumerate(halo_waits(t)):
+        for d, copy in enumerate(halo_copies(t, True)):
             pl.when(near[d][0])(copy.wait)
-        return [
-            halo[t, d, :, :] + dot16(dht_ref[d, :, :], solved_of(near[d][1])) for d in range(4)
-        ]
-
+        return jnp.concatenate(
+            [halo[t, d, :, :] + dot16(dht_ref[d, :, :], solved_of(near[d][1])) for d in range(4)], axis=0
+        )
+
+    load_rhs.wait()
+    start_coarse(0, rhs_ref[...])
+
+    load_rows.wait()
     for d in range(4):
         wanted = jnp.transpose(jnp.broadcast_to(rows_ref[d : d + 1, :].astype(f32), (ov, ov)))
         wanted = jnp.concatenate([wanted] * (rows // ov), axis=1).astype(jnp.int32)
         hot = wanted == lax.broadcasted_iota(jnp.int32, (ov, rows), 1)
         pick_ref[d * ov : (d + 1) * ov, :] = jnp.where(hot, 1.0, 0.0).astype(bf16)
-
-    q0, coarse0 = local_prec(rhs_ref[...])
-    pending = exchange(0, q0, coarse0, jnp.zeros((k, src), f32), True)
-    for copy in extra_a:
-        copy.wait()
-    extra_b = [
-        remote(extra.at[me_x], extra.at[me_x], eb_send.at[i], eb_recv.at[i], (other, me_y))
-        for i, other in enumerate(along_x)
-    ]
-    for copy in extra_b:
-        copy.start()
-
     for d in range(4):
         halo_d_out[d, :, :] = lax.dot_general(
             defl, pick_ref[d * ov : (d + 1) * ov, :], (((1,), (1,)), ((), ())), preferred_element_type=f32
@@ -334,7 +347,21 @@
         copy = remote(halo_d_out.at[d], halo_d.at[d ^ 1], hd_send.at[d], hd_recv.at[d ^ 1], near[d][1])
         pl.when(near[d][0])(copy.start)
 
-    sb_ref[:, 0:rows] = schur_ref[...]
+    forward_coarse(0)
+    wait(extra_a)
+    extra_b = to_columns(extra.at[me_x], eb_send, eb_recv)
+    start(extra_b)
+
+    def column_of(ref):
+        return jnp.transpose(jnp.broadcast_to(ref[...], (src, rows)))
+
+    td_ref[...] = column_of(tdiag_ref)
+    q0 = local_prec(rhs_ref[...])
+    send_halo(0, q0)
+
+    load_sdiag.wait()
+    sd_ref[...] = column_of(sdiag_ref)
+    load_coup.wait()
     for d in range(4):
         hot = rows_ref[d : d + 1, :] == lax.broadcasted_iota(jnp.int32, (rows, ov), 0)
         spread = dot16(jnp.where(hot, -1.0, 0.0).astype(bf16), coup_ref[d, :, :])
@@ -344,23 +371,32 @@
         arrival = remote(halo_d_out.at[d], halo_d.at[d], hd_send.at[d], hd_recv.at[d], near[d][1])
         pl.when(near[d][0])(arrival.wait)
         dht_ref[d, :, :] = jnp.transpose(jnp.concatenate([halo_d[d, :, :]] * 3, axis=0)).astype(bf16)
-
-    for copy in extra_b:
-        copy.wait()
-    inverse = jnp.concatenate([extra[a, b, 0:k, :] for a in range(gx) for b in range(gy)], axis=0)
-    gram_ref[...] = jnp.concatenate([extra[a, b, k : 2 * k, :] for a in range(gx) for b in range(gy)], axis=0)
+    load_cmap.wait()
     order = cmap_ref[...] == lax.broadcasted_iota(jnp.int32, (nc, nc), 0)
-    cp_ref[...] = wide_dot(inverse, jnp.where(order, 1.0, 0.0))
-
-    for copy in pending:
-        copy.wait()
-    coarse_all, dq_all, _ = gathered(0)
-    solved, projected = solve(coarse_all, dq_all)
+    order = jnp.where(order, 1.0, 0.0).astype(bf16)
+
+    wait(extra_b)
+    blocks = [(a, b) for a in range(gx) for b in range(gy)]
+    inverse = jnp.concatenate([extra[a, b, :, 0:nc] for a, b in blocks], axis=0)
+    inverse = sum(dot16(piece, order) for piece in reversed(pieces(inverse)))
+    gram = jnp.concatenate([extra[a, b, :, nc:] for a, b in blocks], axis=0)
+    row = lax.broadcasted_iota(jnp.int32, (src, nc), 0)
+    column = lax.broadcasted_iota(jnp.int32, (src, nc), 1)
+    repeat = jnp.where(row == column % k, 1.0, 0.0).astype(bf16)
+    gram = sum(dot16(piece, repeat) for piece in reversed(pieces(gram)))
+    row = lax.broadcasted_iota(jnp.int32, (nc, nc), 0)
+    column = lax.broadcasted_iota(jnp.int32, (nc, nc), 1)
+    gram = jnp.where(row // k == column // k, gram, 0.0)
+    both_ref[0:nc, :] = six(inverse, True)
+    both_ref[nc:, :] = six(wide_dot(gram, inverse), True)
+
+    solved, _, projected = solve(0)
     e_ref[...] = projected
     d_ref[...] = q0 + dot16(dt_ref[...], solved_of((me_x, me_y)))
-    dh_ref[...] = jnp.concatenate(halo_mapped(0), axis=0)
+    dh_ref[...] = halo_mapped(0)
     x_ref[...] = jnp.zeros_like(x_ref)
     xh_ref[...] = jnp.zeros_like(xh_ref)
+    load_schur.wait()
 
     def schur(field_ref, margin_ref):
         v_ref[0:rows, :] = field_ref[...].astype(bf16)
@@ -370,8 +406,10 @@
     def iteration(step, carry):
         t = step + 1
         more = t < iters
-        q, coarse = local_prec(schur(d_ref, dh_ref).astype(bf16))
-        sums = jnp.concatenate(
+        rounded = schur(d_ref, dh_ref).astype(bf16)
+        start_coarse(t, rounded)
+        q = local_prec(rounded)
+        sum_a[t, me_y, :, :] = jnp.concatenate(
             [
                 jnp.sum(q * d_ref[...], axis=0, keepdims=True),
                 jnp.sum(q * q, axis=0, keepdims=True),
@@ -379,13 +417,25 @@
             ],
             axis=0,
         )
-        for copy in exchange(t, q, coarse, sums, more):
-            copy.wait()
-        coarse_all, dq_all, total = gathered(t)
-        solved, projected = solve(coarse_all, dq_all)
-        numer = total[0:1] + jnp.sum(solved * e_ref[...], axis=0, keepdims=True)
-        denom = total[1:2] + jnp.sum(solved * (dq_all + projected), axis=0, keepdims=True)
-        alpha = numer / denom
+        first = to_lines(sum_a.at[t, me_y], sa_send.at[t], sa_recv.at[t])
+        start(first)
+        forward_coarse(t)
+        wait(first)
+        total = sum_a[t, 0, :, :]
+        for b in range(1, gy):
+            total = total + sum_a[t, b, :, :]
+        sum_b[t, me_x, :, :] = total
+        second = to_columns(sum_b.at[t, me_x], sb_send.at[t], sb_recv.at[t])
+        start(second)
+        pl.when(more)(lambda: send_halo(t, q))
+        solved, dq_all, projected = solve(t)
+        numer = jnp.sum(solved * e_ref[...], axis=0, keepdims=True)
+        denom = jnp.sum(solved * (dq_all + projected), axis=0, keepdims=True)
+        wait(second)
+        total = sum_b[t, 0, :, :]
+        for a in range(1, gx):
+            total = total + sum_b[t, a, :, :]
+        alpha = (total[0:1] + numer) / (total[1:2] + denom)
         x_ref[...] += alpha * d_ref[...]
         xh_ref[...] += alpha * dh_ref[...]
 
@@ -393,7 +443,7 @@
         def _():
             d_ref[...] -= alpha * (q + dot16(dt_ref[...], solved_of((me_x, me_y))))
             e_ref[...] -= alpha * projected
-            dh_ref[...] -= alpha * jnp.concatenate(halo_mapped(t), axis=0)
+            dh_ref[...] -= alpha * halo_mapped(t)
 
         return carry
 
@@ -413,9 +463,18 @@
     x, residual = pl.pallas_call(
         functools.partial(kernel, gx, gy),
         out_shape=[jax.ShapeDtypeStruct((rows, src), f32)] * 2,
-        in_specs=[pl.BlockSpec(memory_space=pltpu.VMEM)] * 10,
+        in_specs=[pl.BlockSpec(memory_space=pl.ANY)] * 10,
         out_specs=[pl.BlockSpec(memory_space=pltpu.VMEM)] * 2,
         scratch_shapes=[
+            vmem((rows, src), bf16),
+            vmem((1, rows), f32),
+            vmem((rows, rows), bf16),
+            vmem((1, rows), f32),
+            vmem((4, ov, ov), bf16),
+            vmem((4, ov), jnp.int32),
+            vmem((k, rows), bf16),
+            vmem((1, nc), jnp.int32),
+            dma((10,)),
             vmem((rows, rows + 4 * ov), bf16),
             vmem((4 * ov, rows), bf16),
             vmem((rows + 4 * ov, src), bf16),
@@ -428,15 +487,20 @@
             vmem((nc, src), f32),
             vmem((rows, 3 * k), bf16),
             vmem((4, ov, 3 * k), bf16),
-            vmem((nc, nc), f32),
-            vmem((nc, nc), f32),
-            vmem((rounds, gy, 3 * k, src), f32),
-            vmem((rounds, gx, (2 * gy + 1) * k, src), f32),
-            vmem((gx, gy, 2 * k, nc), f32),
-            vmem((rounds, 4, ov, src), f32),
+            vmem((2 * nc, 6 * nc), bf16),
+            vmem((4 * k, rows), bf16),
+            vmem((rounds, gx, gy, 2 * k, src), f32),
+            vmem((rounds, gy, k, src), f32),
+            vmem((rounds, gx, k, src), f32),
+            vmem((gx, gy, k, nc + src), f32),
+            vmem((ITERS, 4, ov, src), f32),
             vmem((4, k, ov), f32),
             vmem((4, k, ov), f32),
-            vmem((rounds, 4, ov, src), f32),
+            vmem((ITERS, 4, ov, src), f32),
+            dma((rounds, gy - 1)),
+            dma((rounds, gy - 1)),
+            dma((rounds, gx - 1)),
+            dma((rounds, gx - 1)),
             dma((rounds, gy - 1)),
             dma((rounds, gy - 1)),
             dma((rounds, gx - 1)),
@@ -445,13 +509,13 @@
             dma((gy - 1,)),
             dma((gx - 1,)),
             dma((gx - 1,)),
-            dma((rounds, 4)),
-            dma((rounds, 4)),
+            dma((ITERS, 4)),
+            dma((ITERS, 4)),
             dma((4,)),
             dma((4,)),
         ],
         compiler_params=pltpu.CompilerParams(
-            collective_id=0, has_side_effects=True, vmem_limit_bytes=48 * 1024 * 1024
+            collective_id=0, has_side_effects=True, vmem_limit_bytes=60 * 1024 * 1024
         ),
         cost_estimate=pl.CostEstimate(flops=4_000_000_000, bytes_accessed=6_000_000, transcendentals=0),
     )(

time: 71.7 us -> 60.2 us (0.84)
  local copies, waits for them, and re-layouts: 10.3 us -> 3.63 us
  Pallas kernels: 60.3 us -> 55.7 us
    unnamed x22 -> x2, local copies, waits for them, and re-layouts: 10.3 us -> 3.63 us
    pallas_call x1, Pallas kernels: 60.3 us -> 55.7 us  [one_kernel(): pl.pallas_call(functools.partial(kernel, gx, gy), out_shape=[jax.ShapeDty...]
where the time goes in v2:
time: 60.2 us; the launch traced here: 60 us
  Pallas kernels  55.7 us (93%)
  local copies, waits for them, and re-layouts  3.63 us (6%)
  between operations  0.64 us (1%)
    pallas_call x1, Pallas kernels, one_kernel(): pl.pallas_call(functools.partial(kernel, gx, gy), out_shape=[jax.ShapeDty...  55.7 us
    unnamed x2, local copies, waits for them, and re-layouts  3.63 us

profile of v2, /device:TPU:0, one launch (start us, length us, event | category | flops | bytes accessed | tf_op | source)
XLA Modules:
  0.0 60.0 jit_solution(3870773080490620966)
XLA Ops:
  0.6 55.7 %shard_map.113 = (f32[896,128]{1,0:T(8,128)}, f32[896,128]{1,0:T(8,128)}) custom-call(bf16[896,128]{1,0:T(8,128)(2,1)} %bitcast.15, bf16[896,896]{1,0:T(8,128)(2,1)} %bitcast.13, f32[1,896]{1,0:T(1,128)} %bitcast.18, bf16[896,896]{1,0:T(8,128)(2,1)} %bitcast.14, f32[1,896]{1,0:T(1,128)} %bitcast.19, bf16[4,128,128]{2,1,0:T(8,128)(2,1)} %bitcast.16, ...), custom_call_target="tpu_custom_call" | custom-call | flops 4000000000 | bytes 6000000 | tf_op jit(solution)/shard_map/pallas_call | solution.py:463
  56.4 1.8 %copy.14 = f32[1,1,896,128]{3,2,1,0:T(8,128)} copy(f32[1,1,896,128]{3,2,1,0:T(8,128)} %bitcast.12) | data formatting | bytes 917504
  58.2 1.8 %copy.15 = f32[1,1,896,128]{3,2,1,0:T(8,128)} copy(f32[1,1,896,128]{3,2,1,0:T(8,128)} %bitcast.11) | data formatting | bytes 917504

commit v3 on v2

--- a/solution.py
+++ b/solution.py
@@ -245,6 +245,33 @@
     def to_columns(ref, send, recv):
         return [remote(ref, ref, send.at[i], recv.at[i], (other, me_y)) for i, other in enumerate(along_x)]
 
+    sibling = me_x + 1 - 2 * lax.rem(me_x, 2)
+    ahead = [lax.rem(me_x + 2 * step, gx) for step in range(1, gx // 2)]
+    behind = [lax.rem(me_x + gx - 2 * step, gx) for step in range(1, gx // 2)]
+
+    def to_chips(ref, send, recv):
+        return [
+            remote(ref.at[me_x], ref.at[me_x], send.at[i], recv.at[i], (other, me_y)) for i, other in enumerate(ahead)
+        ]
+
+    def to_sibling(ref, send, recv):
+        last = gx // 2 - 1
+        return [
+            remote(ref.at[x], ref.at[x], send.at[last + i], recv.at[last + i], (sibling, me_y))
+            for i, x in enumerate([me_x] + behind)
+        ]
+
+    def spread(ref, send, recv):
+        start(to_chips(ref, send, recv))
+        to_sibling(ref, send, recv)[0].start()
+
+    def collect(ref, send, recv):
+        own, *passed = to_sibling(ref, send, recv)
+        for arrival, copy in zip(to_chips(ref, send, recv), passed):
+            arrival.wait()
+            copy.start()
+        wait([own] + passed)
+
     def start(copies):
         for copy in copies:
             copy.start()
@@ -273,22 +300,18 @@
         [defl_wide] + [piece.astype(f32) for piece in pieces(with_trace)], axis=0
     ).astype(bf16)
 
-    def coarse_copies(t):
-        return (
-            to_lines(main.at[t, me_x, me_y], a_send.at[t], a_recv.at[t]),
-            to_columns(main.at[t, me_x], b_send.at[t], b_recv.at[t]),
-        )
+    def coarse_lines(t):
+        return to_lines(main.at[t, me_x, me_y], a_send.at[t], a_recv.at[t])
 
     def start_coarse(t, rounded):
         out = dot16(small_ref[...], rounded)
         main[t, me_x, me_y, 0:k, :] = out[0:k]
         main[t, me_x, me_y, k : 2 * k, :] = out[k : 2 * k] + (out[2 * k : 3 * k] + out[3 * k : 4 * k])
-        start(coarse_copies(t)[0])
+        start(coarse_lines(t))
 
     def forward_coarse(t):
-        first, second = coarse_copies(t)
-        wait(first)
-        start(second)
+        wait(coarse_lines(t))
+        spread(main.at[t], b_send.at[t], b_recv.at[t])
 
     def local_prec(rounded):
         return td_ref[...] * rounded.astype(f32) + dot16(trace_ref[...], rounded)
@@ -313,7 +336,7 @@
             pl.when(near[d][0])(copy.start)
 
     def solve(t):
-        wait(coarse_copies(t)[1])
+        collect(main.at[t], b_send.at[t], b_recv.at[t])
         coarse_all = jnp.concatenate([main[t, a, b, 0:k, :] for a in range(gx) for b in range(gy)], axis=0)
         dq_all = jnp.concatenate([main[t, a, b, k : 2 * k, :] for a in range(gx) for b in range(gy)], axis=0)
         both = dot16(both_ref[...], six(coarse_all, False))
@@ -349,8 +372,7 @@
 
     forward_coarse(0)
     wait(extra_a)
-    extra_b = to_columns(extra.at[me_x], eb_send, eb_recv)
-    start(extra_b)
+    spread(extra, eb_send, eb_recv)
 
     def column_of(ref):
         return jnp.transpose(jnp.broadcast_to(ref[...], (src, rows)))
@@ -364,8 +386,8 @@
     load_coup.wait()
     for d in range(4):
         hot = rows_ref[d : d + 1, :] == lax.broadcasted_iota(jnp.int32, (rows, ov), 0)
-        spread = dot16(jnp.where(hot, -1.0, 0.0).astype(bf16), coup_ref[d, :, :])
-        sb_ref[:, rows + d * ov : rows + (d + 1) * ov] = spread.astype(bf16)
+        scattered = dot16(jnp.where(hot, -1.0, 0.0).astype(bf16), coup_ref[d, :, :])
+        sb_ref[:, rows + d * ov : rows + (d + 1) * ov] = scattered.astype(bf16)
     dt_ref[...] = jnp.transpose(jnp.concatenate([defl_wide] * 3, axis=0)).astype(bf16)
     for d in range(4):
         arrival = remote(halo_d_out.at[d], halo_d.at[d], hd_send.at[d], hd_recv.at[d], near[d][1])
@@ -375,7 +397,7 @@
     order = cmap_ref[...] == lax.broadcasted_iota(jnp.int32, (nc, nc), 0)
     order = jnp.where(order, 1.0, 0.0).astype(bf16)
 
-    wait(extra_b)
+    collect(extra, eb_send, eb_recv)
     blocks = [(a, b) for a in range(gx) for b in range(gy)]
     inverse = jnp.concatenate([extra[a, b, :, 0:nc] for a, b in blocks], axis=0)
     inverse = sum(dot16(piece, order) for piece in reversed(pieces(inverse)))
@@ -449,6 +471,24 @@
 
     lax.fori_loop(0, iters, iteration, 0)
     res_ref[...] = rhs_ref[...].astype(f32) - schur(x_ref, xh_ref)
+
+
+def hand_on(x_in, res_in, x_out, res_out, held, in_sem, out_sem):
+    half = x_in.shape[0] // 2
+    parts = [(i, j) for j in range(2) for i in range(2)]
+    inward, outward = [], []
+    for i, j in parts:
+        source, target = (x_in, res_in)[i], (x_out, res_out)[i]
+        here = pl.ds(j * half, half)
+        inward.append(pltpu.make_async_copy(source.at[here], held.at[i, j], in_sem.at[i, j]))
+        outward.append(pltpu.make_async_copy(held.at[i, j], target.at[here], out_sem.at[i, j]))
+    for copy in inward:
+        copy.start()
+    for arrival, copy in zip(inward, outward):
+        arrival.wait()
+        copy.start()
+    for copy in outward:
+        copy.wait()
 
 
 def one_kernel(gx, gy, *args):
@@ -530,11 +570,20 @@
         inverse,
         coarse_map[None],
     )
+    x, residual = pl.pallas_call(
+        hand_on,
+        out_shape=[jax.ShapeDtypeStruct((rows, src), f32)] * 2,
+        in_specs=[pl.BlockSpec(memory_space=pl.ANY)] * 2,
+        out_specs=[pl.BlockSpec(memory_space=pl.ANY)] * 2,
+        compiler_params=pltpu.CompilerParams(vmem_limit_bytes=60 * 1024 * 1024),
+        scratch_shapes=[vmem((2, 2, rows // 2, src), f32), dma((2, 2)), dma((2, 2))],
+        cost_estimate=pl.CostEstimate(flops=0, bytes_accessed=16 * rows * src, transcendentals=0),
+    )(x, residual)
     return x[None, None], residual[None, None]
 
 
 def plan(gx, gy, *args):
-    if args[8].shape[1] <= REPLICATED_COARSE:
+    if gx % 2 == 0 and args[8].shape[1] <= REPLICATED_COARSE:
         return one_kernel(gx, gy, *args)
     return shards(*args)
 

time: 60.2 us -> 57.9 us (0.962)
  local copies, waits for them, and re-layouts: 3.63 us -> 0 us
  Pallas kernels: 55.7 us -> 57 us
    unnamed x2 -> x0, local copies, waits for them, and re-layouts: 3.63 us -> none
    pallas_call x0 -> x1, Pallas kernels: none -> 2.04 us  [one_kernel(): pl.pallas_call(hand_on, out_shape=[jax.ShapeDtypeStruct((rows, src), f32)...]
    pallas_call x1, Pallas kernels: 55.7 us -> 55 us  [one_kernel(): pl.pallas_call(functools.partial(kernel, gx, gy), out_shape=[jax.ShapeDty...]
where the time goes in v3:
time: 57.9 us; the launch traced here: 57.6 us
  Pallas kernels  57 us (98%)
  between operations  0.64 us (1%)
    pallas_call x1, Pallas kernels, one_kernel(): pl.pallas_call(functools.partial(kernel, gx, gy), out_shape=[jax.ShapeDty...  55 us
    pallas_call x1, Pallas kernels, one_kernel(): pl.pallas_call(hand_on, out_shape=[jax.ShapeDtypeStruct((rows, src), f32)...  2.04 us

profile of v3, /device:TPU:0, one launch (start us, length us, event | category | flops | bytes accessed | tf_op | source)
XLA Modules:
  0.0 57.6 jit_solution(16380501383408058142)
XLA Ops:
  0.6 55.0 %shard_map.113 = (f32[896,128]{1,0:T(8,128)}, f32[896,128]{1,0:T(8,128)}) custom-call(bf16[896,128]{1,0:T(8,128)(2,1)} %bitcast.15, bf16[896,896]{1,0:T(8,128)(2,1)} %bitcast.11, f32[1,896]{1,0:T(1,128)} %bitcast.18, bf16[896,896]{1,0:T(8,128)(2,1)} %bitcast.12, f32[1,896]{1,0:T(1,128)} %bitcast.19, bf16[4,128,128]{2,1,0:T(8,128)(2,1)} %bitcast.16, ...), custom_call_target="tpu_custom_call" | custom-call | flops 4000000000 | bytes 6000000 | tf_op jit(solution)/shard_map/pallas_call | solution.py:503
  55.6 2.0 %shard_map.114 = (f32[896,128]{1,0:T(8,128)}, f32[896,128]{1,0:T(8,128)}) custom-call(f32[896,128]{1,0:T(8,128)} %get-tuple-element.6.x_in, f32[896,128]{1,0:T(8,128)} %get-tuple-element.7.res_in), custom_call_target="tpu_custom_call" | custom-call | bytes 1835008 | tf_op jit(solution)/shard_map/pallas_call | solution.py:573

commit v4 on v3

--- a/solution.py
+++ b/solution.py
@@ -158,6 +158,8 @@
     dh_ref,
     xh_ref,
     e_ref,
+    last_ref,
+    alpha_ref,
     solved_ref,
     dt_ref,
     dht_ref,
@@ -254,23 +256,28 @@
             remote(ref.at[me_x], ref.at[me_x], send.at[i], recv.at[i], (other, me_y)) for i, other in enumerate(ahead)
         ]
 
+    def to_sibling_one(ref, send, recv, i):
+        at = gx // 2 - 1 + i
+        block = ref.at[me_x if i == 0 else behind[i - 1]]
+        return remote(block, block, send.at[at], recv.at[at], (sibling, me_y))
+
     def to_sibling(ref, send, recv):
-        last = gx // 2 - 1
-        return [
-            remote(ref.at[x], ref.at[x], send.at[last + i], recv.at[last + i], (sibling, me_y))
-            for i, x in enumerate([me_x] + behind)
-        ]
+        return [to_sibling_one(ref, send, recv, i) for i in range(gx // 2)]
 
     def spread(ref, send, recv):
         start(to_chips(ref, send, recv))
-        to_sibling(ref, send, recv)[0].start()
+        to_sibling_one(ref, send, recv, 0).start()
+
+    def pass_on(ref, send, recv):
+        arrivals = to_chips(ref, send, recv)
+        for arrival in arrivals:
+            arrival.wait_send()
+        for i, arrival in enumerate(arrivals):
+            arrival.wait_recv()
+            to_sibling_one(ref, send, recv, i + 1).start()
 
     def collect(ref, send, recv):
-        own, *passed = to_sibling(ref, send, recv)
-        for arrival, copy in zip(to_chips(ref, send, recv), passed):
-            arrival.wait()
-            copy.start()
-        wait([own] + passed)
+        wait(to_sibling(ref, send, recv))
 
     def start(copies):
         for copy in copies:
@@ -278,7 +285,9 @@
 
     def wait(copies):
         for copy in copies:
-            copy.wait()
+            copy.wait_send()
+        for copy in copies:
+            copy.wait_recv()
 
     load_defl.wait()
     defl = defl_ref[...]
@@ -335,6 +344,10 @@
         for d, copy in enumerate(halo_copies(t, False)):
             pl.when(near[d][0])(copy.start)
 
+    def wait_halo(t):
+        for d, copy in enumerate(halo_copies(t, True)):
+            pl.when(near[d][0])(copy.wait)
+
     def solve(t):
         collect(main.at[t], b_send.at[t], b_recv.at[t])
         coarse_all = jnp.concatenate([main[t, a, b, 0:k, :] for a in range(gx) for b in range(gy)], axis=0)
@@ -348,14 +361,14 @@
         return jnp.concatenate(pieces(solved_ref[pl.ds(pl.multiple_of(at, k), k), :]), axis=0)
 
     def halo_mapped(t):
-        for d, copy in enumerate(halo_copies(t, True)):
-            pl.when(near[d][0])(copy.wait)
         return jnp.concatenate(
             [halo[t, d, :, :] + dot16(dht_ref[d, :, :], solved_of(near[d][1])) for d in range(4)], axis=0
         )
 
     load_rhs.wait()
     start_coarse(0, rhs_ref[...])
+    wait(extra_a)
+    spread(extra, eb_send, eb_recv)
 
     load_rows.wait()
     for d in range(4):
@@ -371,8 +384,6 @@
         pl.when(near[d][0])(copy.start)
 
     forward_coarse(0)
-    wait(extra_a)
-    spread(extra, eb_send, eb_recv)
 
     def column_of(ref):
         return jnp.transpose(jnp.broadcast_to(ref[...], (src, rows)))
@@ -380,6 +391,7 @@
     td_ref[...] = column_of(tdiag_ref)
     q0 = local_prec(rhs_ref[...])
     send_halo(0, q0)
+    pass_on(extra, eb_send, eb_recv)
 
     load_sdiag.wait()
     sd_ref[...] = column_of(sdiag_ref)
@@ -393,6 +405,7 @@
         arrival = remote(halo_d_out.at[d], halo_d.at[d], hd_send.at[d], hd_recv.at[d], near[d][1])
         pl.when(near[d][0])(arrival.wait)
         dht_ref[d, :, :] = jnp.transpose(jnp.concatenate([halo_d[d, :, :]] * 3, axis=0)).astype(bf16)
+    pass_on(main.at[0], b_send.at[0], b_recv.at[0])
     load_cmap.wait()
     order = cmap_ref[...] == lax.broadcasted_iota(jnp.int32, (nc, nc), 0)
     order = jnp.where(order, 1.0, 0.0).astype(bf16)
@@ -412,28 +425,34 @@
     both_ref[0:nc, :] = six(inverse, True)
     both_ref[nc:, :] = six(wide_dot(gram, inverse), True)
 
+    x_ref[...] = jnp.zeros_like(x_ref)
+    xh_ref[...] = jnp.zeros_like(xh_ref)
+    d_ref[0, :, :] = jnp.zeros((rows, src), f32)
+    dh_ref[0, :, :] = jnp.zeros((4 * ov, src), f32)
+    alpha_ref[...] = jnp.zeros_like(alpha_ref)
+    last_ref[...] = jnp.zeros_like(last_ref)
+    load_schur.wait()
+    wait_halo(0)
     solved, _, projected = solve(0)
     e_ref[...] = projected
-    d_ref[...] = q0 + dot16(dt_ref[...], solved_of((me_x, me_y)))
-    dh_ref[...] = halo_mapped(0)
-    x_ref[...] = jnp.zeros_like(x_ref)
-    xh_ref[...] = jnp.zeros_like(xh_ref)
-    load_schur.wait()
-
-    def schur(field_ref, margin_ref):
-        v_ref[0:rows, :] = field_ref[...].astype(bf16)
-        v_ref[rows:, :] = margin_ref[...].astype(bf16)
+    d_ref[1, :, :] = q0 + dot16(dt_ref[...], solved_of((me_x, me_y)))
+    dh_ref[1, :, :] = halo_mapped(0)
+
+    def schur(field, margin):
+        v_ref[0:rows, :] = field.astype(bf16)
+        v_ref[rows:, :] = margin.astype(bf16)
         return sd_ref[...] * v_ref[0:rows, :].astype(f32) + dot16(sb_ref[...], v_ref[...])
 
     def iteration(step, carry):
         t = step + 1
+        now, other = t % 2, (t + 1) % 2
         more = t < iters
-        rounded = schur(d_ref, dh_ref).astype(bf16)
+        rounded = schur(d_ref[now], dh_ref[now]).astype(bf16)
         start_coarse(t, rounded)
         q = local_prec(rounded)
         sum_a[t, me_y, :, :] = jnp.concatenate(
             [
-                jnp.sum(q * d_ref[...], axis=0, keepdims=True),
+                jnp.sum(q * d_ref[now], axis=0, keepdims=True),
                 jnp.sum(q * q, axis=0, keepdims=True),
                 jnp.zeros((k - 2, src), f32),
             ],
@@ -441,6 +460,9 @@
         )
         first = to_lines(sum_a.at[t, me_y], sa_send.at[t], sa_recv.at[t])
         start(first)
+        x_ref[...] += alpha_ref[0:1, :] * d_ref[other]
+        xh_ref[...] += alpha_ref[0:1, :] * dh_ref[other]
+        e_ref[...] -= alpha_ref[0:1, :] * last_ref[...]
         forward_coarse(t)
         wait(first)
         total = sum_a[t, 0, :, :]
@@ -450,6 +472,8 @@
         second = to_columns(sum_b.at[t, me_x], sb_send.at[t], sb_recv.at[t])
         start(second)
         pl.when(more)(lambda: send_halo(t, q))
+        pass_on(main.at[t], b_send.at[t], b_recv.at[t])
+        pl.when(more)(lambda: wait_halo(t))
         solved, dq_all, projected = solve(t)
         numer = jnp.sum(solved * e_ref[...], axis=0, keepdims=True)
         denom = jnp.sum(solved * (dq_all + projected), axis=0, keepdims=True)
@@ -458,19 +482,21 @@
         for a in range(1, gx):
             total = total + sum_b[t, a, :, :]
         alpha = (total[0:1] + numer) / (total[1:2] + denom)
-        x_ref[...] += alpha * d_ref[...]
-        xh_ref[...] += alpha * dh_ref[...]
+        alpha_ref[...] = jnp.broadcast_to(alpha, alpha_ref.shape)
+        last_ref[...] = projected
 
         @pl.when(more)
         def _():
-            d_ref[...] -= alpha * (q + dot16(dt_ref[...], solved_of((me_x, me_y))))
-            e_ref[...] -= alpha * projected
-            dh_ref[...] -= alpha * halo_mapped(t)
+            d_ref[other, :, :] = d_ref[now] - alpha * (q + dot16(dt_ref[...], solved_of((me_x, me_y))))
+            dh_ref[other, :, :] = dh_ref[now] - alpha * halo_mapped(t)
 
         return carry
 
     lax.fori_loop(0, iters, iteration, 0)
-    res_ref[...] = rhs_ref[...].astype(f32) - schur(x_ref, xh_ref)
+    x = x_ref[...] + alpha_ref[0:1, :] * d_ref[iters % 2]
+    xh = xh_ref[...] + alpha_ref[0:1, :] * dh_ref[iters % 2]
+    x_ref[...] = x
+    res_ref[...] = rhs_ref[...].astype(f32) - schur(x, xh)
 
 
 def hand_on(x_in, res_in, x_out, res_out, held, in_sem, out_sem):
@@ -520,10 +546,12 @@
             vmem((rows + 4 * ov, src), bf16),
             vmem((rows, src), f32),
             vmem((rows, src), f32),
-            vmem((rows, src), f32),
-            vmem((4 * ov, src), f32),
+            vmem((2, rows, src), f32),
+            vmem((2, 4 * ov, src), f32),
             vmem((4 * ov, src), f32),
             vmem((nc, src), f32),
+            vmem((nc, src), f32),
+            vmem((8, src), f32),
             vmem((nc, src), f32),
             vmem((rows, 3 * k), bf16),
             vmem((4, ov, 3 * k), bf16),

time: 57.9 us -> 55.2 us (0.953)
  Pallas kernels: 57 us -> 54.3 us
    pallas_call x1, Pallas kernels: 55 us -> 52.3 us  [one_kernel(): pl.pallas_call(functools.partial(kernel, gx, gy), out_shape=[jax.ShapeDty...]
where the time goes in v4:
time: 55.2 us; the launch traced here: 55 us
  Pallas kernels  54.3 us (98%)
  between operations  0.64 us (1%)
    pallas_call x1, Pallas kernels, one_kernel(): pl.pallas_call(functools.partial(kernel, gx, gy), out_shape=[jax.ShapeDty...  52.3 us
    pallas_call x1, Pallas kernels, one_kernel(): pl.pallas_call(hand_on, out_shape=[jax.ShapeDtypeStruct((rows, src), f32)...  2.04 us

profile of v4, /device:TPU:0, one launch (start us, length us, event | category | flops | bytes accessed | tf_op | source)
XLA Modules:
  0.0 55.0 jit_solution(6051130856703981440)
XLA Ops:
  0.6 52.3 %shard_map.113 = (f32[896,128]{1,0:T(8,128)}, f32[896,128]{1,0:T(8,128)}) custom-call(bf16[896,128]{1,0:T(8,128)(2,1)} %bitcast.15, bf16[896,896]{1,0:T(8,128)(2,1)} %bitcast.11, f32[1,896]{1,0:T(1,128)} %bitcast.18, bf16[896,896]{1,0:T(8,128)(2,1)} %bitcast.12, f32[1,896]{1,0:T(1,128)} %bitcast.19, bf16[4,128,128]{2,1,0:T(8,128)(2,1)} %bitcast.16, ...), custom_call_target="tpu_custom_call" | custom-call | flops 4000000000 | bytes 6000000 | tf_op jit(solution)/shard_map/pallas_call | solution.py:529
  52.9 2.0 %shard_map.114 = (f32[896,128]{1,0:T(8,128)}, f32[896,128]{1,0:T(8,128)}) custom-call(f32[896,128]{1,0:T(8,128)} %get-tuple-element.6.x_in, f32[896,128]{1,0:T(8,128)} %get-tuple-element.7.res_in), custom_call_target="tpu_custom_call" | custom-call | bytes 1835008 | tf_op jit(solution)/shard_map/pallas_call | solution.py:601

commit v5 on v4

--- a/solution.py
+++ b/solution.py
@@ -93,7 +93,7 @@
 
 
 MESH = pl.DeviceIdType.MESH
-REPLICATED_COARSE = 512
+LARGEST_COARSE = 512
 
 
 def wide_dot(left, right):
@@ -165,8 +165,9 @@
     dht_ref,
     both_ref,
     small_ref,
+    mapped_ref,
     main,
-    sum_a,
+    tail,
     sum_b,
     extra,
     halo,
@@ -183,8 +184,8 @@
     sb_recv,
     ea_send,
     ea_recv,
-    eb_send,
-    eb_recv,
+    en_send,
+    en_recv,
     h_send,
     h_recv,
     hd_send,
@@ -204,7 +205,7 @@
         return copy
 
     load_defl = load(0, defl_hbm, defl_ref)
-    load_cinv = load(1, cinv_hbm, extra.at[me_x, me_y, :, pl.ds(0, nc)])
+    load_cinv = load(1, cinv_hbm, extra.at[me_y, :, pl.ds(0, nc)])
     load_tdiag = load(2, tdiag_hbm, tdiag_ref)
     load_rhs = load(3, rhs_hbm, rhs_ref)
     load_trace = load(4, trace_hbm, trace_ref)
@@ -229,6 +230,8 @@
         def _():
             halo[:, d, :, :] = jnp.zeros((iters, ov, src), f32)
             halo_d[d, :, :] = jnp.zeros((k, ov), f32)
+            if d < 2:
+                extra[gy + d, :, :] = jnp.zeros((k, nc + src), f32)
 
     barrier = pltpu.get_barrier_semaphore()
     for other in along_x:
@@ -247,38 +250,6 @@
     def to_columns(ref, send, recv):
         return [remote(ref, ref, send.at[i], recv.at[i], (other, me_y)) for i, other in enumerate(along_x)]
 
-    sibling = me_x + 1 - 2 * lax.rem(me_x, 2)
-    ahead = [lax.rem(me_x + 2 * step, gx) for step in range(1, gx // 2)]
-    behind = [lax.rem(me_x + gx - 2 * step, gx) for step in range(1, gx // 2)]
-
-    def to_chips(ref, send, recv):
-        return [
-            remote(ref.at[me_x], ref.at[me_x], send.at[i], recv.at[i], (other, me_y)) for i, other in enumerate(ahead)
-        ]
-
-    def to_sibling_one(ref, send, recv, i):
-        at = gx // 2 - 1 + i
-        block = ref.at[me_x if i == 0 else behind[i - 1]]
-        return remote(block, block, send.at[at], recv.at[at], (sibling, me_y))
-
-    def to_sibling(ref, send, recv):
-        return [to_sibling_one(ref, send, recv, i) for i in range(gx // 2)]
-
-    def spread(ref, send, recv):
-        start(to_chips(ref, send, recv))
-        to_sibling_one(ref, send, recv, 0).start()
-
-    def pass_on(ref, send, recv):
-        arrivals = to_chips(ref, send, recv)
-        for arrival in arrivals:
-            arrival.wait_send()
-        for i, arrival in enumerate(arrivals):
-            arrival.wait_recv()
-            to_sibling_one(ref, send, recv, i + 1).start()
-
-    def collect(ref, send, recv):
-        wait(to_sibling(ref, send, recv))
-
     def start(copies):
         for copy in copies:
             copy.start()
@@ -293,14 +264,21 @@
     defl = defl_ref[...]
     defl_wide = defl.astype(f32)
     padded = jnp.concatenate([defl_wide, jnp.zeros((src - k, rows), f32)], axis=0).astype(bf16)
-    extra[me_x, me_y, :, nc:] = lax.dot_general(
+    extra[me_y, :, nc:] = lax.dot_general(
         defl, padded, (((1,), (1,)), ((), ())), preferred_element_type=f32
     )
     load_cinv.wait()
     pl.semaphore_wait(barrier, gx + gy - 2)
 
-    extra_a = to_lines(extra.at[me_x, me_y], ea_send, ea_recv)
+    extra_a = to_lines(extra.at[me_y], ea_send, ea_recv)
     start(extra_a)
+
+    def extra_near(d, arriving):
+        slot = d if arriving else d ^ 1
+        return remote(extra.at[me_y], extra.at[gy + slot], en_send.at[d], en_recv.at[slot], near[d][1])
+
+    for d in range(2):
+        pl.when(near[d][0])(extra_near(d, False).start)
 
     load_tdiag.wait()
     load_trace.wait()
@@ -314,13 +292,19 @@
 
     def start_coarse(t, rounded):
         out = dot16(small_ref[...], rounded)
-        main[t, me_x, me_y, 0:k, :] = out[0:k]
-        main[t, me_x, me_y, k : 2 * k, :] = out[k : 2 * k] + (out[2 * k : 3 * k] + out[3 * k : 4 * k])
+        main[t, me_x, me_y, :, :] = out[0:k]
         start(coarse_lines(t))
+        tail[t, me_y, 0:k, :] = out[k : 2 * k] + (out[2 * k : 3 * k] + out[3 * k : 4 * k])
+
+    def coarse_columns(t):
+        return to_columns(main.at[t, me_x], b_send.at[t], b_recv.at[t])
 
     def forward_coarse(t):
         wait(coarse_lines(t))
-        spread(main.at[t], b_send.at[t], b_recv.at[t])
+        start(coarse_columns(t))
+
+    def tail_lines(t):
+        return to_lines(tail.at[t, me_y], sa_send.at[t], sa_recv.at[t])
 
     def local_prec(rounded):
         return td_ref[...] * rounded.astype(f32) + dot16(trace_ref[...], rounded)
@@ -348,27 +332,31 @@
         for d, copy in enumerate(halo_copies(t, True)):
             pl.when(near[d][0])(copy.wait)
 
+    line = gy * k
+    blocks = line + 2 * k
+
     def solve(t):
-        collect(main.at[t], b_send.at[t], b_recv.at[t])
-        coarse_all = jnp.concatenate([main[t, a, b, 0:k, :] for a in range(gx) for b in range(gy)], axis=0)
-        dq_all = jnp.concatenate([main[t, a, b, k : 2 * k, :] for a in range(gx) for b in range(gy)], axis=0)
+        wait(coarse_columns(t))
+        coarse_all = jnp.concatenate([main[t, a, b, :, :] for a in range(gx) for b in range(gy)], axis=0)
         both = dot16(both_ref[...], six(coarse_all, False))
-        solved_ref[...] = both[0:nc]
-        return both[0:nc], dq_all, dq_all + both[nc:]
-
-    def solved_of(device):
-        at = (device[0] * gy + device[1]) * k
+        solved_ref[...] = both[0:blocks]
+        dq = jnp.concatenate([tail[t, b, 0:k, :] for b in range(gy)], axis=0)
+        return both[0:line], dq, dq + both[blocks:]
+
+    solved_at = [line, line + k, near[2][1][1] * k, near[3][1][1] * k]
+
+    def solved_of(at):
         return jnp.concatenate(pieces(solved_ref[pl.ds(pl.multiple_of(at, k), k), :]), axis=0)
 
     def halo_mapped(t):
         return jnp.concatenate(
-            [halo[t, d, :, :] + dot16(dht_ref[d, :, :], solved_of(near[d][1])) for d in range(4)], axis=0
+            [halo[t, d, :, :] + dot16(dht_ref[d, :, :], solved_of(solved_at[d])) for d in range(4)], axis=0
         )
 
     load_rhs.wait()
     start_coarse(0, rhs_ref[...])
-    wait(extra_a)
-    spread(extra, eb_send, eb_recv)
+    tail[0, me_y, k:, :] = jnp.zeros((k, src), f32)
+    start(tail_lines(0))
 
     load_rows.wait()
     for d in range(4):
@@ -391,7 +379,6 @@
     td_ref[...] = column_of(tdiag_ref)
     q0 = local_prec(rhs_ref[...])
     send_halo(0, q0)
-    pass_on(extra, eb_send, eb_recv)
 
     load_sdiag.wait()
     sd_ref[...] = column_of(sdiag_ref)
@@ -405,25 +392,26 @@
         arrival = remote(halo_d_out.at[d], halo_d.at[d], hd_send.at[d], hd_recv.at[d], near[d][1])
         pl.when(near[d][0])(arrival.wait)
         dht_ref[d, :, :] = jnp.transpose(jnp.concatenate([halo_d[d, :, :]] * 3, axis=0)).astype(bf16)
-    pass_on(main.at[0], b_send.at[0], b_recv.at[0])
     load_cmap.wait()
     order = cmap_ref[...] == lax.broadcasted_iota(jnp.int32, (nc, nc), 0)
     order = jnp.where(order, 1.0, 0.0).astype(bf16)
 
-    collect(extra, eb_send, eb_recv)
-    blocks = [(a, b) for a in range(gx) for b in range(gy)]
-    inverse = jnp.concatenate([extra[a, b, :, 0:nc] for a, b in blocks], axis=0)
+    wait(extra_a)
+    for d in range(2):
+        pl.when(near[d][0])(extra_near(d, True).wait)
+    inverse = jnp.concatenate([extra[b, :, 0:nc] for b in range(gy + 2)], axis=0)
     inverse = sum(dot16(piece, order) for piece in reversed(pieces(inverse)))
-    gram = jnp.concatenate([extra[a, b, :, nc:] for a, b in blocks], axis=0)
-    row = lax.broadcasted_iota(jnp.int32, (src, nc), 0)
-    column = lax.broadcasted_iota(jnp.int32, (src, nc), 1)
-    repeat = jnp.where(row == column % k, 1.0, 0.0).astype(bf16)
+    gram = jnp.concatenate([extra[b, :, nc:] for b in range(gy)], axis=0)
+    row = lax.broadcasted_iota(jnp.int32, (src, src), 0)
+    column = lax.broadcasted_iota(jnp.int32, (src, src), 1)
+    repeat = jnp.where((row == column % k) & (column < line), 1.0, 0.0).astype(bf16)
     gram = sum(dot16(piece, repeat) for piece in reversed(pieces(gram)))
-    row = lax.broadcasted_iota(jnp.int32, (nc, nc), 0)
-    column = lax.broadcasted_iota(jnp.int32, (nc, nc), 1)
+    row = lax.broadcasted_iota(jnp.int32, (line, src), 0)
+    column = lax.broadcasted_iota(jnp.int32, (line, src), 1)
     gram = jnp.where(row // k == column // k, gram, 0.0)
-    both_ref[0:nc, :] = six(inverse, True)
-    both_ref[nc:, :] = six(wide_dot(gram, inverse), True)
+    lined = jnp.concatenate([inverse[0:line], jnp.zeros((src - line, nc), f32)], axis=0)
+    both_ref[0:blocks, :] = six(inverse, True)
+    both_ref[blocks:, :] = six(wide_dot(gram, lined), True)
 
     x_ref[...] = jnp.zeros_like(x_ref)
     xh_ref[...] = jnp.zeros_like(xh_ref)
@@ -433,9 +421,10 @@
     last_ref[...] = jnp.zeros_like(last_ref)
     load_schur.wait()
     wait_halo(0)
+    wait(tail_lines(0))
     solved, _, projected = solve(0)
     e_ref[...] = projected
-    d_ref[1, :, :] = q0 + dot16(dt_ref[...], solved_of((me_x, me_y)))
+    d_ref[1, :, :] = q0 + dot16(dt_ref[...], solved_of(me_y * k))
     dh_ref[1, :, :] = halo_mapped(0)
 
     def schur(field, margin):
@@ -450,7 +439,7 @@
         rounded = schur(d_ref[now], dh_ref[now]).astype(bf16)
         start_coarse(t, rounded)
         q = local_prec(rounded)
-        sum_a[t, me_y, :, :] = jnp.concatenate(
+        tail[t, me_y, k:, :] = jnp.concatenate(
             [
                 jnp.sum(q * d_ref[now], axis=0, keepdims=True),
                 jnp.sum(q * q, axis=0, keepdims=True),
@@ -458,37 +447,41 @@
             ],
             axis=0,
         )
-        first = to_lines(sum_a.at[t, me_y], sa_send.at[t], sa_recv.at[t])
-        start(first)
+        start(tail_lines(t))
         x_ref[...] += alpha_ref[0:1, :] * d_ref[other]
         xh_ref[...] += alpha_ref[0:1, :] * dh_ref[other]
         e_ref[...] -= alpha_ref[0:1, :] * last_ref[...]
         forward_coarse(t)
-        wait(first)
-        total = sum_a[t, 0, :, :]
+        pl.when(more)(lambda: send_halo(t, q))
+        wait(tail_lines(t))
+        pl.when(more)(lambda: wait_halo(t))
+        solved, dq, projected = solve(t)
+        total = tail[t, 0, k:, :]
         for b in range(1, gy):
-            total = total + sum_a[t, b, :, :]
-        sum_b[t, me_x, :, :] = total
+            total = total + tail[t, b, k:, :]
+        numer = total[0:1] + jnp.sum(solved * e_ref[...], axis=0, keepdims=True)
+        denom = total[1:2] + jnp.sum(solved * (dq + projected), axis=0, keepdims=True)
+        sum_b[t, me_x, :, :] = jnp.concatenate([numer, denom, jnp.zeros((k - 2, src), f32)], axis=0)
         second = to_columns(sum_b.at[t, me_x], sb_send.at[t], sb_recv.at[t])
         start(second)
-        pl.when(more)(lambda: send_halo(t, q))
-        pass_on(main.at[t], b_send.at[t], b_recv.at[t])
-        pl.when(more)(lambda: wait_halo(t))
-        solved, dq_all, projected = solve(t)
-        numer = jnp.sum(solved * e_ref[...], axis=0, keepdims=True)
-        denom = jnp.sum(solved * (dq_all + projected), axis=0, keepdims=True)
+        last_ref[...] = projected
+
+        @pl.when(more)
+        def _():
+            mapped_ref[0:rows, :] = q + dot16(dt_ref[...], solved_of(me_y * k))
+            mapped_ref[rows:, :] = halo_mapped(t)
+
         wait(second)
         total = sum_b[t, 0, :, :]
         for a in range(1, gx):
             total = total + sum_b[t, a, :, :]
-        alpha = (total[0:1] + numer) / (total[1:2] + denom)
+        alpha = total[0:1] / total[1:2]
         alpha_ref[...] = jnp.broadcast_to(alpha, alpha_ref.shape)
-        last_ref[...] = projected
 
         @pl.when(more)
         def _():
-            d_ref[other, :, :] = d_ref[now] - alpha * (q + dot16(dt_ref[...], solved_of((me_x, me_y))))
-            dh_ref[other, :, :] = dh_ref[now] - alpha * halo_mapped(t)
+            d_ref[other, :, :] = d_ref[now] - alpha * mapped_ref[0:rows, :]
+            dh_ref[other, :, :] = dh_ref[now] - alpha * mapped_ref[rows:, :]
 
         return carry
 
@@ -549,18 +542,19 @@
             vmem((2, rows, src), f32),
             vmem((2, 4 * ov, src), f32),
             vmem((4 * ov, src), f32),
-            vmem((nc, src), f32),
-            vmem((nc, src), f32),
+            vmem((gy * k, src), f32),
+            vmem((gy * k, src), f32),
             vmem((8, src), f32),
-            vmem((nc, src), f32),
+            vmem(((gy + 2) * k, src), f32),
             vmem((rows, 3 * k), bf16),
             vmem((4, ov, 3 * k), bf16),
-            vmem((2 * nc, 6 * nc), bf16),
+            vmem(((2 * gy + 2) * k, 6 * nc), bf16),
             vmem((4 * k, rows), bf16),
-            vmem((rounds, gx, gy, 2 * k, src), f32),
-            vmem((rounds, gy, k, src), f32),
+            vmem((rows + 4 * ov, src), f32),
+            vmem((rounds, gx, gy, k, src), f32),
+            vmem((rounds, gy, 2 * k, src), f32),
             vmem((rounds, gx, k, src), f32),
-            vmem((gx, gy, k, nc + src), f32),
+            vmem((gy + 2, k, nc + src), f32),
             vmem((ITERS, 4, ov, src), f32),
             vmem((4, k, ov), f32),
             vmem((4, k, ov), f32),
@@ -575,8 +569,8 @@
             dma((rounds, gx - 1)),
             dma((gy - 1,)),
             dma((gy - 1,)),
-            dma((gx - 1,)),
-            dma((gx - 1,)),
+            dma((2,)),
+            dma((2,)),
             dma((ITERS, 4)),
             dma((ITERS, 4)),
             dma((4,)),
@@ -611,7 +605,7 @@
 
 
 def plan(gx, gy, *args):
-    if gx % 2 == 0 and args[8].shape[1] <= REPLICATED_COARSE:
+    if args[8].shape[1] <= LARGEST_COARSE:
         return one_kernel(gx, gy, *args)
     return shards(*args)
 

time: 55.2 us -> 57.8 us (1.047)
  Pallas kernels: 54.3 us -> 56.9 us
    pallas_call x1, Pallas kernels: 52.3 us -> 54.9 us  [one_kernel(): pl.pallas_call(functools.partial(kernel, gx, gy), out_shape=[jax.ShapeDty...]
where the time goes in v5:
time: 57.8 us; the launch traced here: 57.5 us
  Pallas kernels  56.9 us (98%)
  between operations  0.64 us (1%)
    pallas_call x1, Pallas kernels, one_kernel(): pl.pallas_call(functools.partial(kernel, gx, gy), out_shape=[jax.ShapeDty...  54.9 us
    pallas_call x1, Pallas kernels, one_kernel(): pl.pallas_call(hand_on, out_shape=[jax.ShapeDtypeStruct((rows, src), f32)...  2.04 us

profile of v5, /device:TPU:0, one launch (start us, length us, event | category | flops | bytes accessed | tf_op | source)
XLA Modules:
  0.0 57.5 jit_solution(1274954849466462561)
XLA Ops:
  0.6 54.9 %shard_map.113 = (f32[896,128]{1,0:T(8,128)}, f32[896,128]{1,0:T(8,128)}) custom-call(bf16[896,128]{1,0:T(8,128)(2,1)} %bitcast.15, bf16[896,896]{1,0:T(8,128)(2,1)} %bitcast.11, f32[1,896]{1,0:T(1,128)} %bitcast.18, bf16[896,896]{1,0:T(8,128)(2,1)} %bitcast.12, f32[1,896]{1,0:T(1,128)} %bitcast.19, bf16[4,128,128]{2,1,0:T(8,128)(2,1)} %bitcast.16, ...), custom_call_target="tpu_custom_call" | custom-call | flops 4000000000 | bytes 6000000 | tf_op jit(solution)/shard_map/pallas_call | solution.py:522
  55.5 2.0 %shard_map.114 = (f32[896,128]{1,0:T(8,128)}, f32[896,128]{1,0:T(8,128)}) custom-call(f32[896,128]{1,0:T(8,128)} %get-tuple-element.6.x_in, f32[896,128]{1,0:T(8,128)} %get-tuple-element.7.res_in), custom_call_target="tpu_custom_call" | custom-call | bytes 1835008 | tf_op jit(solution)/shard_map/pallas_call | solution.py:595

commit v6 on v4

--- a/solution.py
+++ b/solution.py
@@ -214,7 +214,13 @@
     load_coup = load(8, coup_hbm, coup_ref)
     load_schur = load(9, schur_hbm, sb_ref.at[:, pl.ds(0, rows)])
 
-    along_x = [lax.rem(me_x + step, gx) for step in range(1, gx)]
+    chips = gx // 2 * gy
+    core = lax.rem(me_x, 2)
+    sibling = me_x + 1 - 2 * core
+    chip = lax.div(me_x, 2) * gy + me_y
+    others = [lax.rem(chip + step, chips) for step in range(1, chips)]
+    others = [(2 * lax.div(other, gy) + core, lax.rem(other, gy)) for other in others]
+    beside = lax.rem(me_x + gx - 1 + 2 * core, gx)
     along_y = [lax.rem(me_y + step, gy) for step in range(1, gy)]
     near = [
         (me_x > 0, (jnp.maximum(me_x - 1, 0), me_y)),
@@ -231,10 +237,8 @@
             halo_d[d, :, :] = jnp.zeros((k, ov), f32)
 
     barrier = pltpu.get_barrier_semaphore()
-    for other in along_x:
-        pl.semaphore_signal(barrier, inc=1, device_id=(other, me_y), device_id_type=MESH)
-    for other in along_y:
-        pl.semaphore_signal(barrier, inc=1, device_id=(me_x, other), device_id_type=MESH)
+    for device in others + [(sibling, me_y), (beside, me_y)]:
+        pl.semaphore_signal(barrier, inc=1, device_id=device, device_id_type=MESH)
 
     def remote(source, target, send, recv, device):
         return pltpu.make_async_remote_copy(
@@ -244,10 +248,13 @@
     def to_lines(ref, send, recv):
         return [remote(ref, ref, send.at[i], recv.at[i], (me_x, other)) for i, other in enumerate(along_y)]
 
-    def to_columns(ref, send, recv):
-        return [remote(ref, ref, send.at[i], recv.at[i], (other, me_y)) for i, other in enumerate(along_x)]
-
-    sibling = me_x + 1 - 2 * lax.rem(me_x, 2)
+    def to_others(ref, send, recv):
+        return [remote(ref.at[chip], ref.at[chip], send, recv, device) for device in others]
+
+    def all_others(ref, send, recv):
+        blocks = ref.at[pl.ds(0, chips - 1)]
+        return remote(blocks, blocks, send, recv, others[0])
+
     ahead = [lax.rem(me_x + 2 * step, gx) for step in range(1, gx // 2)]
     behind = [lax.rem(me_x + gx - 2 * step, gx) for step in range(1, gx // 2)]
 
@@ -297,7 +304,7 @@
         defl, padded, (((1,), (1,)), ((), ())), preferred_element_type=f32
     )
     load_cinv.wait()
-    pl.semaphore_wait(barrier, gx + gy - 2)
+    pl.semaphore_wait(barrier, chips + 1)
 
     extra_a = to_lines(extra.at[me_x, me_y], ea_send, ea_recv)
     start(extra_a)
@@ -309,18 +316,20 @@
         [defl_wide] + [piece.astype(f32) for piece in pieces(with_trace)], axis=0
     ).astype(bf16)
 
-    def coarse_lines(t):
-        return to_lines(main.at[t, me_x, me_y], a_send.at[t], a_recv.at[t])
-
     def start_coarse(t, rounded):
         out = dot16(small_ref[...], rounded)
-        main[t, me_x, me_y, 0:k, :] = out[0:k]
-        main[t, me_x, me_y, k : 2 * k, :] = out[k : 2 * k] + (out[2 * k : 3 * k] + out[3 * k : 4 * k])
-        start(coarse_lines(t))
+        main[t, core, chip, 0:k, :] = out[0:k]
+        main[t, core, chip, k : 2 * k, :] = out[k : 2 * k] + (out[2 * k : 3 * k] + out[3 * k : 4 * k])
+        start(to_others(main.at[t, core], a_send.at[t], a_recv.at[t]))
+
+    def swap_coarse(t):
+        return remote(main.at[t, core], main.at[t, core], b_send.at[t], b_recv.at[t], (sibling, me_y))
 
     def forward_coarse(t):
-        wait(coarse_lines(t))
-        spread(main.at[t], b_send.at[t], b_recv.at[t])
+        arrived = all_others(main.at[t, core], a_send.at[t], a_recv.at[t])
+        arrived.wait_send()
+        arrived.wait_recv()
+        swap_coarse(t).start()
 
     def local_prec(rounded):
         return td_ref[...] * rounded.astype(f32) + dot16(trace_ref[...], rounded)
@@ -348,10 +357,12 @@
         for d, copy in enumerate(halo_copies(t, True)):
             pl.when(near[d][0])(copy.wait)
 
+    blocks = [(a, b) for a in range(gx) for b in range(gy)]
+
     def solve(t):
-        collect(main.at[t], b_send.at[t], b_recv.at[t])
-        coarse_all = jnp.concatenate([main[t, a, b, 0:k, :] for a in range(gx) for b in range(gy)], axis=0)
-        dq_all = jnp.concatenate([main[t, a, b, k : 2 * k, :] for a in range(gx) for b in range(gy)], axis=0)
+        swap_coarse(t).wait()
+        coarse_all = jnp.concatenate([main[t, a % 2, a // 2 * gy + b, 0:k, :] for a, b in blocks], axis=0)
+        dq_all = jnp.concatenate([main[t, a % 2, a // 2 * gy + b, k : 2 * k, :] for a, b in blocks], axis=0)
         both = dot16(both_ref[...], six(coarse_all, False))
         solved_ref[...] = both[0:nc]
         return both[0:nc], dq_all, dq_all + both[nc:]
@@ -382,8 +393,6 @@
         )
         copy = remote(halo_d_out.at[d], halo_d.at[d ^ 1], hd_send.at[d], hd_recv.at[d ^ 1], near[d][1])
         pl.when(near[d][0])(copy.start)
-
-    forward_coarse(0)
 
     def column_of(ref):
         return jnp.transpose(jnp.broadcast_to(ref[...], (src, rows)))
@@ -405,13 +414,12 @@
         arrival = remote(halo_d_out.at[d], halo_d.at[d], hd_send.at[d], hd_recv.at[d], near[d][1])
         pl.when(near[d][0])(arrival.wait)
         dht_ref[d, :, :] = jnp.transpose(jnp.concatenate([halo_d[d, :, :]] * 3, axis=0)).astype(bf16)
-    pass_on(main.at[0], b_send.at[0], b_recv.at[0])
+    forward_coarse(0)
     load_cmap.wait()
     order = cmap_ref[...] == lax.broadcasted_iota(jnp.int32, (nc, nc), 0)
     order = jnp.where(order, 1.0, 0.0).astype(bf16)
 
     collect(extra, eb_send, eb_recv)
-    blocks = [(a, b) for a in range(gx) for b in range(gy)]
     inverse = jnp.concatenate([extra[a, b, :, 0:nc] for a, b in blocks], axis=0)
     inverse = sum(dot16(piece, order) for piece in reversed(pieces(inverse)))
     gram = jnp.concatenate([extra[a, b, :, nc:] for a, b in blocks], axis=0)
@@ -450,7 +458,7 @@
         rounded = schur(d_ref[now], dh_ref[now]).astype(bf16)
         start_coarse(t, rounded)
         q = local_prec(rounded)
-        sum_a[t, me_y, :, :] = jnp.concatenate(
+        sum_a[t, chip, :, :] = jnp.concatenate(
             [
                 jnp.sum(q * d_ref[now], axis=0, keepdims=True),
                 jnp.sum(q * q, axis=0, keepdims=True),
@@ -458,29 +466,27 @@
             ],
             axis=0,
         )
-        first = to_lines(sum_a.at[t, me_y], sa_send.at[t], sa_recv.at[t])
-        start(first)
+        start(to_others(sum_a.at[t], sa_send.at[t], sa_recv.at[t]))
         x_ref[...] += alpha_ref[0:1, :] * d_ref[other]
         xh_ref[...] += alpha_ref[0:1, :] * dh_ref[other]
         e_ref[...] -= alpha_ref[0:1, :] * last_ref[...]
+        pl.when(more)(lambda: send_halo(t, q))
         forward_coarse(t)
-        wait(first)
+        arrived = all_others(sum_a.at[t], sa_send.at[t], sa_recv.at[t])
+        arrived.wait_send()
+        arrived.wait_recv()
         total = sum_a[t, 0, :, :]
-        for b in range(1, gy):
-            total = total + sum_a[t, b, :, :]
-        sum_b[t, me_x, :, :] = total
-        second = to_columns(sum_b.at[t, me_x], sb_send.at[t], sb_recv.at[t])
-        start(second)
-        pl.when(more)(lambda: send_halo(t, q))
-        pass_on(main.at[t], b_send.at[t], b_recv.at[t])
+        for i in range(1, chips):
+            total = total + sum_a[t, i, :, :]
+        sum_b[t, core, :, :] = total
+        swap = remote(sum_b.at[t, core], sum_b.at[t, core], sb_send.at[t], sb_recv.at[t], (sibling, me_y))
+        swap.start()
         pl.when(more)(lambda: wait_halo(t))
         solved, dq_all, projected = solve(t)
         numer = jnp.sum(solved * e_ref[...], axis=0, keepdims=True)
         denom = jnp.sum(solved * (dq_all + projected), axis=0, keepdims=True)
-        wait(second)
-        total = sum_b[t, 0, :, :]
-        for a in range(1, gx):
-            total = total + sum_b[t, a, :, :]
+        swap.wait()
+        total = sum_b[t, 0, :, :] + sum_b[t, 1, :, :]
         alpha = (total[0:1] + numer) / (total[1:2] + denom)
         alpha_ref[...] = jnp.broadcast_to(alpha, alpha_ref.shape)
         last_ref[...] = projected
@@ -557,22 +563,22 @@
             vmem((4, ov, 3 * k), bf16),
             vmem((2 * nc, 6 * nc), bf16),
             vmem((4 * k, rows), bf16),
-            vmem((rounds, gx, gy, 2 * k, src), f32),
-            vmem((rounds, gy, k, src), f32),
-            vmem((rounds, gx, k, src), f32),
+            vmem((rounds, 2, gx // 2 * gy, 2 * k, src), f32),
+            vmem((rounds, gx // 2 * gy, k, src), f32),
+            vmem((rounds, 2, k, src), f32),
             vmem((gx, gy, k, nc + src), f32),
             vmem((ITERS, 4, ov, src), f32),
             vmem((4, k, ov), f32),
             vmem((4, k, ov), f32),
             vmem((ITERS, 4, ov, src), f32),
-            dma((rounds, gy - 1)),
-            dma((rounds, gy - 1)),
-            dma((rounds, gx - 1)),
-            dma((rounds, gx - 1)),
-            dma((rounds, gy - 1)),
-            dma((rounds, gy - 1)),
-            dma((rounds, gx - 1)),
-            dma((rounds, gx - 1)),
+            dma((rounds,)),
+            dma((rounds,)),
+            dma((rounds,)),
+            dma((rounds,)),
+            dma((rounds,)),
+            dma((rounds,)),
+            dma((rounds,)),
+            dma((rounds,)),
             dma((gy - 1,)),
             dma((gy - 1,)),
             dma((gx - 1,)),

time: 55.2 us -> 52.8 us (0.957)
  Pallas kernels: 54.3 us -> 51.9 us
    pallas_call x1, Pallas kernels: 52.3 us -> 49.9 us  [one_kernel(): pl.pallas_call(functools.partial(kernel, gx, gy), out_shape=[jax.ShapeDty...]
where the time goes in v6:
time: 52.8 us; the launch traced here: 52.6 us
  Pallas kernels  51.9 us (98%)
  between operations  0.64 us (1%)
    pallas_call x1, Pallas kernels, one_kernel(): pl.pallas_call(functools.partial(kernel, gx, gy), out_shape=[jax.ShapeDty...  49.9 us
    pallas_call x1, Pallas kernels, one_kernel(): pl.pallas_call(hand_on, out_shape=[jax.ShapeDtypeStruct((rows, src), f32)...  2.04 us

profile of v6, /device:TPU:0, one launch (start us, length us, event | category | flops | bytes accessed | tf_op | source)
XLA Modules:
  0.0 52.6 jit_solution(14649550602741816)
XLA Ops:
  0.6 49.9 %shard_map.113 = (f32[896,128]{1,0:T(8,128)}, f32[896,128]{1,0:T(8,128)}) custom-call(bf16[896,128]{1,0:T(8,128)(2,1)} %bitcast.15, bf16[896,896]{1,0:T(8,128)(2,1)} %bitcast.11, f32[1,896]{1,0:T(1,128)} %bitcast.18, bf16[896,896]{1,0:T(8,128)(2,1)} %bitcast.12, f32[1,896]{1,0:T(1,128)} %bitcast.19, bf16[4,128,128]{2,1,0:T(8,128)(2,1)} %bitcast.16, ...), custom_call_target="tpu_custom_call" | custom-call | flops 4000000000 | bytes 6000000 | tf_op jit(solution)/shard_map/pallas_call | solution.py:535
  50.5 2.0 %shard_map.114 = (f32[896,128]{1,0:T(8,128)}, f32[896,128]{1,0:T(8,128)}) custom-call(f32[896,128]{1,0:T(8,128)} %get-tuple-element.6.x_in, f32[896,128]{1,0:T(8,128)} %get-tuple-element.7.res_in), custom_call_target="tpu_custom_call" | custom-call | bytes 1835008 | tf_op jit(solution)/shard_map/pallas_call | solution.py:607

commit v7 on v6

--- a/solution.py
+++ b/solution.py
@@ -166,8 +166,7 @@
     both_ref,
     small_ref,
     main,
-    sum_a,
-    sum_b,
+    tail,
     extra,
     halo,
     halo_d,
@@ -318,18 +317,32 @@
 
     def start_coarse(t, rounded):
         out = dot16(small_ref[...], rounded)
-        main[t, core, chip, 0:k, :] = out[0:k]
-        main[t, core, chip, k : 2 * k, :] = out[k : 2 * k] + (out[2 * k : 3 * k] + out[3 * k : 4 * k])
+        main[t, core, chip, :, :] = out[0:k]
+        tail[t, core, chip, 0:k, :] = out[k : 2 * k] + (out[2 * k : 3 * k] + out[3 * k : 4 * k])
         start(to_others(main.at[t, core], a_send.at[t], a_recv.at[t]))
+
+    def start_tail(t, numer, denom):
+        tail[t, core, chip, k : k + 1, :] = numer
+        tail[t, core, chip, k + 1 : k + 2, :] = denom
+        start(to_others(tail.at[t, core], sa_send.at[t], sa_recv.at[t]))
 
     def swap_coarse(t):
         return remote(main.at[t, core], main.at[t, core], b_send.at[t], b_recv.at[t], (sibling, me_y))
 
-    def forward_coarse(t):
-        arrived = all_others(main.at[t, core], a_send.at[t], a_recv.at[t])
+    def swap_tail(t):
+        return remote(tail.at[t, core], tail.at[t, core], sb_send.at[t], sb_recv.at[t], (sibling, me_y))
+
+    def forward(ref, send, recv, swap):
+        arrived = all_others(ref, send, recv)
         arrived.wait_send()
         arrived.wait_recv()
-        swap_coarse(t).start()
+        swap.start()
+
+    def forward_coarse(t):
+        forward(main.at[t, core], a_send.at[t], a_recv.at[t], swap_coarse(t))
+
+    def forward_tail(t):
+        forward(tail.at[t, core], sa_send.at[t], sa_recv.at[t], swap_tail(t))
 
     def local_prec(rounded):
         return td_ref[...] * rounded.astype(f32) + dot16(trace_ref[...], rounded)
@@ -361,11 +374,15 @@
 
     def solve(t):
         swap_coarse(t).wait()
-        coarse_all = jnp.concatenate([main[t, a % 2, a // 2 * gy + b, 0:k, :] for a, b in blocks], axis=0)
-        dq_all = jnp.concatenate([main[t, a % 2, a // 2 * gy + b, k : 2 * k, :] for a, b in blocks], axis=0)
+        coarse_all = jnp.concatenate([main[t, a % 2, a // 2 * gy + b, :, :] for a, b in blocks], axis=0)
         both = dot16(both_ref[...], six(coarse_all, False))
         solved_ref[...] = both[0:nc]
-        return both[0:nc], dq_all, dq_all + both[nc:]
+        return both[0:nc], both[nc:]
+
+    def tail_of(t, gram_solved):
+        swap_tail(t).wait()
+        dq_all = jnp.concatenate([tail[t, a % 2, a // 2 * gy + b, 0:k, :] for a, b in blocks], axis=0)
+        return dq_all, dq_all + gram_solved
 
     def solved_of(device):
         at = (device[0] * gy + device[1]) * k
@@ -378,6 +395,7 @@
 
     load_rhs.wait()
     start_coarse(0, rhs_ref[...])
+    start_tail(0, jnp.zeros((1, src), f32), jnp.zeros((1, src), f32))
     wait(extra_a)
     spread(extra, eb_send, eb_recv)
 
@@ -415,6 +433,7 @@
         pl.when(near[d][0])(arrival.wait)
         dht_ref[d, :, :] = jnp.transpose(jnp.concatenate([halo_d[d, :, :]] * 3, axis=0)).astype(bf16)
     forward_coarse(0)
+    forward_tail(0)
     load_cmap.wait()
     order = cmap_ref[...] == lax.broadcasted_iota(jnp.int32, (nc, nc), 0)
     order = jnp.where(order, 1.0, 0.0).astype(bf16)
@@ -441,8 +460,8 @@
     last_ref[...] = jnp.zeros_like(last_ref)
     load_schur.wait()
     wait_halo(0)
-    solved, _, projected = solve(0)
-    e_ref[...] = projected
+    _, projected = solve(0)
+    e_ref[...] = tail_of(0, projected)[1]
     d_ref[1, :, :] = q0 + dot16(dt_ref[...], solved_of((me_x, me_y)))
     dh_ref[1, :, :] = halo_mapped(0)
 
@@ -458,35 +477,21 @@
         rounded = schur(d_ref[now], dh_ref[now]).astype(bf16)
         start_coarse(t, rounded)
         q = local_prec(rounded)
-        sum_a[t, chip, :, :] = jnp.concatenate(
-            [
-                jnp.sum(q * d_ref[now], axis=0, keepdims=True),
-                jnp.sum(q * q, axis=0, keepdims=True),
-                jnp.zeros((k - 2, src), f32),
-            ],
-            axis=0,
-        )
-        start(to_others(sum_a.at[t], sa_send.at[t], sa_recv.at[t]))
+        start_tail(t, jnp.sum(q * d_ref[now], axis=0, keepdims=True), jnp.sum(q * q, axis=0, keepdims=True))
         x_ref[...] += alpha_ref[0:1, :] * d_ref[other]
         xh_ref[...] += alpha_ref[0:1, :] * dh_ref[other]
         e_ref[...] -= alpha_ref[0:1, :] * last_ref[...]
         pl.when(more)(lambda: send_halo(t, q))
         forward_coarse(t)
-        arrived = all_others(sum_a.at[t], sa_send.at[t], sa_recv.at[t])
-        arrived.wait_send()
-        arrived.wait_recv()
-        total = sum_a[t, 0, :, :]
-        for i in range(1, chips):
-            total = total + sum_a[t, i, :, :]
-        sum_b[t, core, :, :] = total
-        swap = remote(sum_b.at[t, core], sum_b.at[t, core], sb_send.at[t], sb_recv.at[t], (sibling, me_y))
-        swap.start()
+        forward_tail(t)
+        solved, gram_solved = solve(t)
         pl.when(more)(lambda: wait_halo(t))
-        solved, dq_all, projected = solve(t)
         numer = jnp.sum(solved * e_ref[...], axis=0, keepdims=True)
+        dq_all, projected = tail_of(t, gram_solved)
         denom = jnp.sum(solved * (dq_all + projected), axis=0, keepdims=True)
-        swap.wait()
-        total = sum_b[t, 0, :, :] + sum_b[t, 1, :, :]
+        total = tail[t, 0, 0, k:, :]
+        for i in range(1, 2 * chips):
+            total = total + tail[t, i // chips, i % chips, k:, :]
         alpha = (total[0:1] + numer) / (total[1:2] + denom)
         alpha_ref[...] = jnp.broadcast_to(alpha, alpha_ref.shape)
         last_ref[...] = projected
@@ -505,21 +510,14 @@
     res_ref[...] = rhs_ref[...].astype(f32) - schur(x, xh)
 
 
-def hand_on(x_in, res_in, x_out, res_out, held, in_sem, out_sem):
-    half = x_in.shape[0] // 2
-    parts = [(i, j) for j in range(2) for i in range(2)]
-    inward, outward = [], []
-    for i, j in parts:
-        source, target = (x_in, res_in)[i], (x_out, res_out)[i]
-        here = pl.ds(j * half, half)
-        inward.append(pltpu.make_async_copy(source.at[here], held.at[i, j], in_sem.at[i, j]))
-        outward.append(pltpu.make_async_copy(held.at[i, j], target.at[here], out_sem.at[i, j]))
-    for copy in inward:
+def hand_on(x_in, res_in, x_out, res_out, sem):
+    copies = [
+        pltpu.make_async_copy(source, target, sem.at[i])
+        for i, (source, target) in enumerate([(x_in, x_out), (res_in, res_out)])
+    ]
+    for copy in copies:
         copy.start()
-    for arrival, copy in zip(inward, outward):
-        arrival.wait()
-        copy.start()
-    for copy in outward:
+    for copy in copies:
         copy.wait()
 
 
@@ -563,9 +561,8 @@
             vmem((4, ov, 3 * k), bf16),
             vmem((2 * nc, 6 * nc), bf16),
             vmem((4 * k, rows), bf16),
-            vmem((rounds, 2, gx // 2 * gy, 2 * k, src), f32),
-            vmem((rounds, gx // 2 * gy, k, src), f32),
-            vmem((rounds, 2, k, src), f32),
+            vmem((rounds, 2, gx // 2 * gy, k, src), f32),
+            vmem((rounds, 2, gx // 2 * gy, k + 2, src), f32),
             vmem((gx, gy, k, nc + src), f32),
             vmem((ITERS, 4, ov, src), f32),
             vmem((4, k, ov), f32),
@@ -610,7 +607,7 @@
         in_specs=[pl.BlockSpec(memory_space=pl.ANY)] * 2,
         out_specs=[pl.BlockSpec(memory_space=pl.ANY)] * 2,
         compiler_params=pltpu.CompilerParams(vmem_limit_bytes=60 * 1024 * 1024),
-        scratch_shapes=[vmem((2, 2, rows // 2, src), f32), dma((2, 2)), dma((2, 2))],
+        scratch_shapes=[dma((2,))],
         cost_estimate=pl.CostEstimate(flops=0, bytes_accessed=16 * rows * src, transcendentals=0),
     )(x, residual)
     return x[None, None], residual[None, None]

time: 52.8 us -> 77.1 us (1.46)
  Pallas kernels: 51.9 us -> 76.2 us
    pallas_call x1, Pallas kernels: 2.04 us -> 28.9 us  [one_kernel(): pl.pallas_call(hand_on, out_shape=[jax.ShapeDtypeStruct((rows, src), f32)...]
    pallas_call x1, Pallas kernels: 49.9 us -> 47.3 us  [one_kernel(): pl.pallas_call(functools.partial(kernel, gx, gy), out_shape=[jax.ShapeDty...]
where the time goes in v7:
time: 77.1 us; the launch traced here: 76.9 us
  Pallas kernels  76.2 us (99%)
    pallas_call x1, Pallas kernels, one_kernel(): pl.pallas_call(functools.partial(kernel, gx, gy), out_shape=[jax.ShapeDty...  47.3 us
    pallas_call x1, Pallas kernels, one_kernel(): pl.pallas_call(hand_on, out_shape=[jax.ShapeDtypeStruct((rows, src), f32)...  28.9 us

profile of v7, /device:TPU:0, one launch (start us, length us, event | category | flops | bytes accessed | tf_op | source)
XLA Modules:
  0.0 76.9 jit_solution(7731935265054458070)
XLA Ops:
  0.6 47.3 %shard_map.113 = (f32[896,128]{1,0:T(8,128)}, f32[896,128]{1,0:T(8,128)}) custom-call(bf16[896,128]{1,0:T(8,128)(2,1)} %bitcast.15, bf16[896,896]{1,0:T(8,128)(2,1)} %bitcast.11, f32[1,896]{1,0:T(1,128)} %bitcast.18, bf16[896,896]{1,0:T(8,128)(2,1)} %bitcast.12, f32[1,896]{1,0:T(1,128)} %bitcast.19, bf16[4,128,128]{2,1,0:T(8,128)(2,1)} %bitcast.16, ...), custom_call_target="tpu_custom_call" | custom-call | flops 4000000000 | bytes 6000000 | tf_op jit(solution)/shard_map/pallas_call | solution.py:533
  47.9 28.9 %shard_map.114 = (f32[896,128]{1,0:T(8,128)}, f32[896,128]{1,0:T(8,128)}) custom-call(f32[896,128]{1,0:T(8,128)} %get-tuple-element.6.x_in, f32[896,128]{1,0:T(8,128)} %get-tuple-element.7.res_in), custom_call_target="tpu_custom_call" | custom-call | bytes 1835008 | tf_op jit(solution)/shard_map/pallas_call | solution.py:604

commit v8 on v7

--- a/solution.py
+++ b/solution.py
@@ -510,14 +510,21 @@
     res_ref[...] = rhs_ref[...].astype(f32) - schur(x, xh)
 
 
-def hand_on(x_in, res_in, x_out, res_out, sem):
-    copies = [
-        pltpu.make_async_copy(source, target, sem.at[i])
-        for i, (source, target) in enumerate([(x_in, x_out), (res_in, res_out)])
-    ]
-    for copy in copies:
+def hand_on(x_in, res_in, x_out, res_out, held, in_sem, out_sem):
+    half = x_in.shape[0] // 2
+    parts = [(i, j) for j in range(2) for i in range(2)]
+    inward, outward = [], []
+    for i, j in parts:
+        source, target = (x_in, res_in)[i], (x_out, res_out)[i]
+        here = pl.ds(j * half, half)
+        inward.append(pltpu.make_async_copy(source.at[here], held.at[i, j], in_sem.at[i, j]))
+        outward.append(pltpu.make_async_copy(held.at[i, j], target.at[here], out_sem.at[i, j]))
+    for copy in inward:
         copy.start()
-    for copy in copies:
+    for arrival, copy in zip(inward, outward):
+        arrival.wait()
+        copy.start()
+    for copy in outward:
         copy.wait()
 
 
@@ -607,7 +614,7 @@
         in_specs=[pl.BlockSpec(memory_space=pl.ANY)] * 2,
         out_specs=[pl.BlockSpec(memory_space=pl.ANY)] * 2,
         compiler_params=pltpu.CompilerParams(vmem_limit_bytes=60 * 1024 * 1024),
-        scratch_shapes=[dma((2,))],
+        scratch_shapes=[vmem((2, 2, rows // 2, src), f32), dma((2, 2)), dma((2, 2))],
         cost_estimate=pl.CostEstimate(flops=0, bytes_accessed=16 * rows * src, transcendentals=0),
     )(x, residual)
     return x[None, None], residual[None, None]

time: 77.1 us -> 50.2 us (0.65)
  Pallas kernels: 76.2 us -> 49.3 us
    pallas_call x1, Pallas kernels: 28.9 us -> 2.04 us  [one_kernel(): pl.pallas_call(hand_on, out_shape=[jax.ShapeDtypeStruct((rows, src), f32)...]
where the time goes in v8:
time: 50.2 us; the launch traced here: 50 us
  Pallas kernels  49.3 us (98%)
  between operations  0.64 us (1%)
    pallas_call x1, Pallas kernels, one_kernel(): pl.pallas_call(functools.partial(kernel, gx, gy), out_shape=[jax.ShapeDty...  47.3 us
    pallas_call x1, Pallas kernels, one_kernel(): pl.pallas_call(hand_on, out_shape=[jax.ShapeDtypeStruct((rows, src), f32)...  2.04 us

profile of v8, /device:TPU:0, one launch (start us, length us, event | category | flops | bytes accessed | tf_op | source)
XLA Modules:
  0.0 50.0 jit_solution(5929702652725095925)
XLA Ops:
  0.6 47.3 %shard_map.113 = (f32[896,128]{1,0:T(8,128)}, f32[896,128]{1,0:T(8,128)}) custom-call(bf16[896,128]{1,0:T(8,128)(2,1)} %bitcast.15, bf16[896,896]{1,0:T(8,128)(2,1)} %bitcast.11, f32[1,896]{1,0:T(1,128)} %bitcast.18, bf16[896,896]{1,0:T(8,128)(2,1)} %bitcast.12, f32[1,896]{1,0:T(1,128)} %bitcast.19, bf16[4,128,128]{2,1,0:T(8,128)(2,1)} %bitcast.16, ...), custom_call_target="tpu_custom_call" | custom-call | flops 4000000000 | bytes 6000000 | tf_op jit(solution)/shard_map/pallas_call | solution.py:540
  47.9 2.0 %shard_map.114 = (f32[896,128]{1,0:T(8,128)}, f32[896,128]{1,0:T(8,128)}) custom-call(f32[896,128]{1,0:T(8,128)} %get-tuple-element.6.x_in, f32[896,128]{1,0:T(8,128)} %get-tuple-element.7.res_in), custom_call_target="tpu_custom_call" | custom-call | bytes 1835008 | tf_op jit(solution)/shard_map/pallas_call | solution.py:611
